TPU v7x, 32 devices: a whole 2x2x4 slice. The times are simulated.
32 devices in a mesh: rep: 2 (over y), fsdp: 16 (over z, x, core).
Axes of the slice: x: 2, y: 2, z: 4, core: 2. Of those that a mesh axis runs over, the one named last changes fastest.
Arguments:
- pixels_a: bfloat16 [32, 3, 160, 160], P(('rep', 'fsdp')), may hold values from -6 to 6
- pixels_b: bfloat16 [32, 3, 240, 240], P(('rep', 'fsdp')), may hold values from -6 to 6
- pixels_c: bfloat16 [32, 3, 384, 384], P(('rep', 'fsdp')), may hold values from -6 to 6
- resize_a: float32 [100, 1024], replicated, may hold values from -0.1875 to 0.1875
- resize_b: float32 [144, 1024], replicated, may hold values from -0.1875 to 0.1875
- resize_c: float32 [256, 1024], replicated, may hold values from -0.1875 to 0.1875
- posmap_a: float32 [256, 49], replicated, may hold values from 0 to 0.08
- posmap_b: float32 [400, 49], replicated, may hold values from 0 to 0.08
- posmap_c: float32 [576, 49], replicated, may hold values from 0 to 0.08
- base_kernel: bfloat16 [3, 1024, 768], P(None, None, 'fsdp'), may hold values from -0.21875 to 0.21875
- patch_bias: bfloat16 [768], P('fsdp'), may hold values from -3 to 3
- posemb: bfloat16 [49, 768], P(None, 'fsdp'), may hold values from -12 to 12
- ln1_gain: bfloat16 [768], P('fsdp'), may hold values from 0.099609375 to 1.8984375
- ln1_bias: bfloat16 [768], P('fsdp'), may hold values from -2 to 2
- qkv_weight: bfloat16 [768, 2304], P('fsdp'), may hold values from -0.21875 to 0.21875
- qv_bias: bfloat16 [2, 768], P(None, 'fsdp'), may hold values from -3 to 3
- out_weight: bfloat16 [768, 768], P('fsdp'), may hold values from -0.875 to 0.875
- out_bias: bfloat16 [768], P('fsdp'), may hold values from -2 to 2
- ln2_gain: bfloat16 [768], P('fsdp'), may hold values from 0.099609375 to 1.8984375
- ln2_bias: bfloat16 [768], P('fsdp'), may hold values from -2 to 2
- up_weight: bfloat16 [768, 3072], P('fsdp'), may hold values from -0.21875 to 0.21875
- up_bias: bfloat16 [3072], P('fsdp'), may hold values from -3 to 3
- down_weight: bfloat16 [3072, 768], P('fsdp'), may hold values from -0.109375 to 0.109375
- down_bias: bfloat16 [768], P('fsdp'), may hold values from -2 to 2
- cotangent_a: bfloat16 [32, 256, 768], P(('rep', 'fsdp')), may hold values from -6 to 6
- cotangent_b: bfloat16 [32, 400, 768], P(('rep', 'fsdp')), may hold values from -6 to 6
- cotangent_c: bfloat16 [32, 576, 768], P(('rep', 'fsdp')), may hold values from -6 to 6
Outputs:
- out_a: bfloat16 [32, 256, 768], P(('rep', 'fsdp'))
- out_b: bfloat16 [32, 400, 768], P(('rep', 'fsdp'))
- out_c: bfloat16 [32, 576, 768], P(('rep', 'fsdp'))
- pixel_grad_a: bfloat16 [32, 3, 160, 160], P(('rep', 'fsdp'))
- pixel_grad_b: bfloat16 [32, 3, 240, 240], P(('rep', 'fsdp'))
- pixel_grad_c: bfloat16 [32, 3, 384, 384], P(('rep', 'fsdp'))
- base_kernel_grad: float32 [3, 1024, 768], P(None, None, 'fsdp')
- patch_bias_grad: float32 [768], P('fsdp')
- posemb_grad: float32 [49, 768], P(None, 'fsdp')
- ln1_gain_grad: float32 [768], P('fsdp')
- ln1_bias_grad: float32 [768], P('fsdp')
- qkv_weight_grad: float32 [768, 2304], P('fsdp')
- qv_bias_grad: float32 [2, 768], P(None, 'fsdp')
- out_weight_grad: float32 [768, 768], P('fsdp')
- out_bias_grad: float32 [768], P('fsdp')
- ln2_gain_grad: float32 [768], P('fsdp')
- ln2_bias_grad: float32 [768], P('fsdp')
- up_weight_grad: float32 [768, 3072], P('fsdp')
- up_bias_grad: float32 [3072], P('fsdp')
- down_weight_grad: float32 [3072, 768], P('fsdp')
- down_bias_grad: float32 [768], P('fsdp')
All inputs are finite; a program needn't handle non-finite values.
Results may differ from a plain program's by a relative error of at most 0.013.
Values may be sent and summed in bfloat16 or wider, within the bound.
No kernel may reach another device: no remote copies, remote signals or barrier semaphores. Data moves between devices by JAX's collectives and lax.ppermute only.
A program may use at most 256 MiB of HBM per device.

v0:
```python
import math

import jax
import jax.numpy as jnp
from jax import lax
from jax.sharding import PartitionSpec as P

HEADS = 12
HEAD = 64
PA = 10
PB = 12
PC = 16


precise = lax.Precision.HIGHEST


def shortened(value):

    def short(part):
        return part.astype(jnp.bfloat16) if part.dtype == jnp.float32 else part

    return jax.tree.map(short, value)


def patchify(pixels, patch_side):
    image_count = pixels.shape[0]
    grid_side = pixels.shape[2] // patch_side
    blocks = pixels.reshape(image_count, 3, grid_side, patch_side, grid_side, patch_side)
    blocks = blocks.transpose(0, 2, 4, 1, 3, 5)
    return blocks.reshape(image_count * grid_side * grid_side, 3 * patch_side * patch_side)


def unpatch(patch_grads, patch_side, image_count, pixel_side):
    grid_side = pixel_side // patch_side
    blocks = patch_grads.reshape(image_count, grid_side, grid_side, 3, patch_side, patch_side)
    blocks = blocks.transpose(0, 3, 1, 4, 2, 5)
    return blocks.reshape(image_count, 3, pixel_side, pixel_side)


def norm_forward(values, gain, shift):
    mean_row = jnp.mean(values, axis=-1, keepdims=True)
    centred = values - mean_row
    inverse = lax.rsqrt(jnp.mean(centred * centred, axis=-1, keepdims=True) + 1e-06)
    unit_rows = centred * inverse
    return (unit_rows * gain + shift, unit_rows, inverse)


def norm_backward(grad_out, unit_rows, inverse, gain):
    grad_unit = grad_out * gain
    inner = jnp.mean(grad_unit * unit_rows, axis=-1, keepdims=True)
    grad_in = inverse * (
        grad_unit - jnp.mean(grad_unit, axis=-1, keepdims=True) - unit_rows * inner
    )
    return (grad_in, jnp.sum(grad_out * unit_rows, axis=0), jnp.sum(grad_out, axis=0))


def split_heads(qkv_rows, model_width):
    token_count = qkv_rows.shape[0]
    queries = qkv_rows[:, :model_width].reshape(token_count, HEADS, HEAD)
    key_rows = qkv_rows[:, model_width : 2 * model_width].reshape(token_count, HEADS, HEAD)
    value_rows = qkv_rows[:, 2 * model_width :].reshape(token_count, HEADS, HEAD)
    return (queries, key_rows, value_rows)


def attend_forward(qkv_rows):
    model_width = qkv_rows.shape[1] // 3
    queries, key_rows, value_rows = split_heads(qkv_rows, model_width)
    scores = jnp.einsum("qhd,khd->hqk", queries, key_rows, preferred_element_type=jnp.float32)
    scores = scores * (1.0 / math.sqrt(HEAD))
    row_top = jnp.max(scores, axis=-1, keepdims=True)
    expo = jnp.exp(scores - row_top)
    row_total = jnp.sum(expo, axis=-1, keepdims=True)
    attention = expo / row_total
    mixed_rows = jnp.einsum(
        "hqk,khd->qhd",
        attention.astype(jnp.bfloat16),
        value_rows,
        preferred_element_type=jnp.float32,
    )
    return (mixed_rows.reshape(qkv_rows.shape[0], model_width), row_top + jnp.log(row_total))


def attend_backward(packed):
    qkv_rows, log_total, grad_mixed = packed
    token_count = qkv_rows.shape[0]
    model_width = qkv_rows.shape[1] // 3
    scale = 1.0 / math.sqrt(HEAD)
    queries, key_rows, value_rows = split_heads(qkv_rows, model_width)
    scores = (
        jnp.einsum("qhd,khd->hqk", queries, key_rows, preferred_element_type=jnp.float32) * scale
    )
    attention = jnp.exp(scores - log_total)
    grad_heads = grad_mixed.reshape(token_count, HEADS, HEAD)
    grad_value = jnp.einsum(
        "hqk,qhd->khd",
        attention.astype(jnp.bfloat16),
        grad_heads,
        preferred_element_type=jnp.float32,
    )
    grad_attention = jnp.einsum(
        "qhd,khd->hqk", grad_heads, value_rows, preferred_element_type=jnp.float32
    )
    inner = jnp.sum(grad_attention * attention, axis=-1, keepdims=True)
    grad_scores = (attention * (grad_attention - inner)).astype(jnp.bfloat16)
    grad_query = (
        jnp.einsum("hqk,khd->qhd", grad_scores, key_rows, preferred_element_type=jnp.float32)
        * scale
    )
    grad_key = (
        jnp.einsum("hqk,qhd->khd", grad_scores, queries, preferred_element_type=jnp.float32) * scale
    )
    return jnp.concatenate(
        [
            grad_query.reshape(token_count, model_width),
            grad_key.reshape(token_count, model_width),
            grad_value.reshape(token_count, model_width),
        ],
        axis=1,
    )


def embed_weights(shards, resize):
    base_kernel, patch_bias, posemb = (shards[0], shards[1], shards[2])
    whole_base, pos_table, patch_shift = (
        lax.all_gather(base_kernel, "fsdp", axis=2, tiled=True),
        lax.all_gather(posemb, "fsdp", axis=1, tiled=True),
        lax.all_gather(patch_bias, "fsdp", axis=0, tiled=True),
    )
    kernel = jnp.einsum(
        "pb,cbd->cpd", resize, whole_base.astype(jnp.float32), precision=precise
    ).astype(jnp.bfloat16)
    return (kernel.reshape(-1, kernel.shape[2]), pos_table, patch_shift)


def attention_weights(shards):
    return (
        lax.all_gather(shards[3], "fsdp", axis=0, tiled=True),
        lax.all_gather(shards[4], "fsdp", axis=0, tiled=True),
        lax.all_gather(shards[5], "fsdp", axis=0, tiled=True),
        lax.all_gather(shards[6], "fsdp", axis=1, tiled=True),
        lax.all_gather(shards[7], "fsdp", axis=0, tiled=True),
        lax.all_gather(shards[8], "fsdp", axis=0, tiled=True),
    )


def feed_weights(shards):
    return (
        lax.all_gather(shards[9], "fsdp", axis=0, tiled=True),
        lax.all_gather(shards[10], "fsdp", axis=0, tiled=True),
        lax.all_gather(shards[11], "fsdp", axis=0, tiled=True),
        lax.all_gather(shards[12], "fsdp", axis=0, tiled=True),
        lax.all_gather(shards[13], "fsdp", axis=0, tiled=True),
        lax.all_gather(shards[14], "fsdp", axis=0, tiled=True),
    )


def run_batch(shards, pixels, resize, posmap, cotangent, patch_side):
    image_count = pixels.shape[0]
    pixel_side = pixels.shape[2]
    token_count = cotangent.shape[1]
    model_width = cotangent.shape[2]
    all_rows = image_count * token_count
    f32 = jnp.float32
    bf16 = jnp.bfloat16
    embed_set = embed_weights(shards, resize)
    kernel, pos_table, patch_shift = embed_set
    patches = patchify(pixels, patch_side)
    positions = jnp.dot(posmap, pos_table.astype(f32), precision=precise)
    embedded = jnp.dot(patches, kernel, preferred_element_type=f32) + patch_shift.astype(f32)
    embedded = (embedded.reshape(image_count, token_count, model_width) + positions).reshape(
        all_rows, model_width
    )
    attn_set = attention_weights(shards)
    attn_gain, attn_shift, w_qkv, b_qv, w_out, b_out = attn_set
    normed_in, unit_in, inverse_in = norm_forward(
        embedded, attn_gain.astype(f32), attn_shift.astype(f32)
    )
    normed_low = normed_in.astype(bf16)
    qv_rows = b_qv.astype(f32)
    bias_three = jnp.concatenate([qv_rows[0], jnp.zeros_like(qv_rows[0]), qv_rows[1]])
    qkv = (jnp.dot(normed_low, w_qkv, preferred_element_type=f32) + bias_three).astype(bf16)
    qkv_images = qkv.reshape(image_count, token_count, 3 * model_width)
    mixed_rows, log_total = lax.map(attend_forward, qkv_images)
    mixed_low = mixed_rows.reshape(all_rows, model_width).astype(bf16)
    middle = embedded + jnp.dot(mixed_low, w_out, preferred_element_type=f32) + b_out.astype(f32)
    feed_set = feed_weights(shards)
    feed_gain, feed_shift, w_up, b_up, w_down, b_down = feed_set
    normed_mid, unit_mid, inverse_mid = norm_forward(
        middle, feed_gain.astype(f32), feed_shift.astype(f32)
    )
    normed_mid_low = normed_mid.astype(bf16)
    up_pre = jnp.dot(normed_mid_low, w_up, preferred_element_type=f32) + b_up.astype(f32)
    gelu_out, gelu_back = jax.vjp(jax.nn.gelu, up_pre)
    act_low = gelu_out.astype(bf16)
    final_rows = middle + jnp.dot(act_low, w_down, preferred_element_type=f32) + b_down.astype(f32)
    result = final_rows.astype(bf16).reshape(image_count, token_count, model_width)
    feed_set = feed_weights(shards)
    feed_gain, feed_shift, w_up, b_up, w_down, b_down = feed_set
    grad_down = cotangent.reshape(all_rows, model_width)
    grad_final = grad_down.astype(f32)
    grad_w_down = jnp.einsum("rk,rd->kd", act_low, grad_down, preferred_element_type=f32)
    grad_b_down = jnp.sum(grad_final, axis=0)
    grad_act = jnp.einsum("rd,kd->rk", grad_down, w_down, preferred_element_type=f32)
    grad_up = gelu_back(grad_act)[0].astype(bf16)
    grad_w_up = jnp.einsum("rk,rd->kd", normed_mid_low, grad_up, preferred_element_type=f32)
    grad_b_up = jnp.sum(grad_up.astype(f32), axis=0)
    grad_normed_mid = jnp.einsum("rd,kd->rk", grad_up, w_up, preferred_element_type=f32)
    grad_mid_part, grad_feed_gain, grad_feed_shift = norm_backward(
        grad_normed_mid, unit_mid, inverse_mid, feed_gain.astype(f32)
    )
    feed_local = (grad_feed_gain, grad_feed_shift, grad_w_up, grad_b_up, grad_w_down, grad_b_down)
    feed_parts = (
        lax.psum_scatter(feed_local[0], "fsdp", scatter_dimension=0, tiled=True),
        lax.psum_scatter(feed_local[1], "fsdp", scatter_dimension=0, tiled=True),
        lax.psum_scatter(feed_local[2], "fsdp", scatter_dimension=0, tiled=True),
        lax.psum_scatter(feed_local[3], "fsdp", scatter_dimension=0, tiled=True),
        lax.psum_scatter(feed_local[4], "fsdp", scatter_dimension=0, tiled=True),
        lax.psum_scatter(feed_local[5], "fsdp", scatter_dimension=0, tiled=True),
    )
    grad_middle = grad_final + grad_mid_part
    attn_set = attention_weights(shards)
    attn_gain, attn_shift, w_qkv, b_qv, w_out, b_out = attn_set
    grad_branch = grad_middle.astype(bf16)
    grad_w_out = jnp.einsum("rk,rd->kd", mixed_low, grad_branch, preferred_element_type=f32)
    grad_b_out = jnp.sum(grad_branch.astype(f32), axis=0)
    grad_mixed = jnp.einsum("rd,kd->rk", grad_branch, w_out, preferred_element_type=f32).astype(
        bf16
    )
    grad_qkv = lax.map(
        attend_backward,
        (qkv_images, log_total, grad_mixed.reshape(image_count, token_count, model_width)),
    )
    grad_qkv_low = grad_qkv.reshape(all_rows, 3 * model_width).astype(bf16)
    grad_w_qkv = jnp.einsum("rk,rd->kd", normed_low, grad_qkv_low, preferred_element_type=f32)
    column_sums = jnp.sum(grad_qkv_low.astype(f32), axis=0)
    grad_b_qv = jnp.stack([column_sums[:model_width], column_sums[2 * model_width :]])
    grad_normed_in = jnp.einsum("rd,kd->rk", grad_qkv_low, w_qkv, preferred_element_type=f32)
    grad_in_part, grad_attn_gain, grad_attn_shift = norm_backward(
        grad_normed_in, unit_in, inverse_in, attn_gain.astype(f32)
    )
    attn_local = (grad_attn_gain, grad_attn_shift, grad_w_qkv, grad_b_qv, grad_w_out, grad_b_out)
    attn_parts = (
        lax.psum_scatter(attn_local[0], "fsdp", scatter_dimension=0, tiled=True),
        lax.psum_scatter(attn_local[1], "fsdp", scatter_dimension=0, tiled=True),
        lax.psum_scatter(attn_local[2], "fsdp", scatter_dimension=0, tiled=True),
        lax.psum_scatter(attn_local[3], "fsdp", scatter_dimension=1, tiled=True),
        lax.psum_scatter(attn_local[4], "fsdp", scatter_dimension=0, tiled=True),
        lax.psum_scatter(attn_local[5], "fsdp", scatter_dimension=0, tiled=True),
    )
    grad_embedded = grad_middle + grad_in_part
    embed_set = embed_weights(shards, resize)
    kernel, pos_table, patch_shift = embed_set
    grad_embed_low = grad_embedded.astype(bf16)
    grad_patches = jnp.einsum("rd,kd->rk", grad_embed_low, kernel, preferred_element_type=f32)
    pixel_grad = unpatch(grad_patches, patch_side, image_count, pixel_side).astype(bf16)
    grad_kernel = jnp.einsum("rk,rd->kd", patches, grad_embed_low, preferred_element_type=f32)
    grad_kernel = grad_kernel.reshape(3, patch_side * patch_side, model_width)
    grad_positions = jnp.sum(grad_embedded.reshape(image_count, token_count, model_width), axis=0)
    grad_table = jnp.einsum("lp,ld->pd", posmap, grad_positions, precision=precise)
    grad_shift = jnp.sum(grad_embedded, axis=0)
    grad_base = jnp.einsum("pb,cpd->cbd", resize, grad_kernel, precision=precise)
    base_part, table_part, shift_part = (
        lax.psum_scatter(grad_base, "fsdp", scatter_dimension=2, tiled=True),
        lax.psum_scatter(grad_table, "fsdp", scatter_dimension=1, tiled=True),
        lax.psum_scatter(grad_shift, "fsdp", scatter_dimension=0, tiled=True),
    )
    shard_grads = (base_part, shift_part, table_part) + tuple(attn_parts) + tuple(feed_parts)
    return (result, pixel_grad, shard_grads)


def body(
    pixels_a,
    pixels_b,
    pixels_c,
    resize_a,
    resize_b,
    resize_c,
    posmap_a,
    posmap_b,
    posmap_c,
    base_kernel,
    patch_bias,
    posemb,
    ln1_gain,
    ln1_bias,
    qkv_weight,
    qv_bias,
    out_weight,
    out_bias,
    ln2_gain,
    ln2_bias,
    up_weight,
    up_bias,
    down_weight,
    down_bias,
    cotangent_a,
    cotangent_b,
    cotangent_c,
):
    shards = (
        base_kernel,
        patch_bias,
        posemb,
        ln1_gain,
        ln1_bias,
        qkv_weight,
        qv_bias,
        out_weight,
        out_bias,
        ln2_gain,
        ln2_bias,
        up_weight,
        up_bias,
        down_weight,
        down_bias,
    )
    batches = (
        (pixels_a, resize_a, posmap_a, cotangent_a, PA),
        (pixels_b, resize_b, posmap_b, cotangent_b, PB),
        (pixels_c, resize_c, posmap_c, cotangent_c, PC),
    )
    results = []
    pixel_grads = []
    totals = None
    for pixels, resize, posmap, cotangent, patch_side in batches:
        result, pixel_grad, shard_grads = run_batch(
            shards, pixels, resize, posmap, cotangent, patch_side
        )
        results.append(result)
        pixel_grads.append(pixel_grad)
        if totals is None:
            totals = shard_grads
        else:
            totals = tuple((first + second for first, second in zip(totals, shard_grads)))
    summed = jax.tree.map(lambda part: part.astype(jnp.float32), lax.psum(shortened(totals), "rep"))
    return tuple(results) + tuple(pixel_grads) + tuple(summed)


def solution(mesh):
    return jax.shard_map(
        body,
        mesh=mesh,
        in_specs=(
            P(("rep", "fsdp"), None, None, None),
            P(("rep", "fsdp"), None, None, None),
            P(("rep", "fsdp"), None, None, None),
            P(),
            P(),
            P(),
            P(),
            P(),
            P(),
            P(None, None, "fsdp"),
            P("fsdp"),
            P(None, "fsdp"),
            P("fsdp"),
            P("fsdp"),
            P("fsdp", None),
            P(None, "fsdp"),
            P("fsdp", None),
            P("fsdp"),
            P("fsdp"),
            P("fsdp"),
            P("fsdp", None),
            P("fsdp"),
            P("fsdp", None),
            P("fsdp"),
            P(("rep", "fsdp"), None, None),
            P(("rep", "fsdp"), None, None),
            P(("rep", "fsdp"), None, None),
        ),
        out_specs=(
            P(("rep", "fsdp"), None, None),
            P(("rep", "fsdp"), None, None),
            P(("rep", "fsdp"), None, None),
            P(("rep", "fsdp"), None, None, None),
            P(("rep", "fsdp"), None, None, None),
            P(("rep", "fsdp"), None, None, None),
            P(None, None, "fsdp"),
            P("fsdp"),
            P(None, "fsdp"),
            P("fsdp"),
            P("fsdp"),
            P("fsdp", None),
            P(None, "fsdp"),
            P("fsdp", None),
            P("fsdp"),
            P("fsdp"),
            P("fsdp"),
            P("fsdp", None),
            P("fsdp"),
            P("fsdp", None),
            P("fsdp"),
        ),
        check_vma=False,
    )
```

profile of v0, /device:TPU:0, one launch (start us, length us, event | category | flops | bytes accessed | tf_op | source)
XLA Modules:
  0.0 1121.9 jit_solution(15258281072271873919)
XLA Ops:
  20.0 64.0 %all-reduce.17 = (bf16[768]{0:T(1024)(128)(2,1)S(1)}, bf16[768]{0:T(1024)(128)(2,1)S(1)}, bf16[768]{0:T(1024)(128)(2,1)S(1)}, bf16[768]{0:T(1024)(128)(2,1)S(1)}...) all-reduce(bf16[768]{0:T(1024)(128)(2,1)S(1)} %dynamic-update-slice, ...), channel_id=1, replica_groups=mesh['rep'=2,'fsdp'=16] {'fsdp'}, use_global_device_ids=true, to_apply=%add | all-reduce | flops 8448 | bytes 33792
  84.0 8.4 reshape.627
  92.4 8.5 copy.163
  101.0 6.6 reshape.628
  107.6 17.1 %all-gather = bf16[16,48,2]{1,2,0:T(2,128)(2,1)S(1)} all-gather(bf16[1,48,2]{1,2,0:T(2,128)(2,1)S(1)} %bitcast.374), channel_id=1, replica_groups=mesh['rep'=2,'fsdp'=16] {'fsdp'}, dimensions={0}, use_global_device_ids=true | all-gather | bytes 3264 | tf_op jit(solution)/shard_map/all_gather | solution.py:141
  129.6 8.5 copy.158
  152.3 19.9 %all_gather.32 = bf16[49,768]{0,1:T(8,128)(2,1)S(1)} all-gather(bf16[49,48]{0,1:T(8,128)(2,1)S(1)} %copy-done.141), channel_id=1, replica_groups=mesh['rep'=2,'fsdp'=16] {'fsdp'}, dimensions={1}, use_global_device_ids=true | all-gather | bytes 79968 | tf_op jit(solution)/shard_map/all_gather | solution.py:127
  172.3 7.4 convolution_convert_fusion.2
  209.2 6.8 fusion.119
  216.0 47.2 %all-gather.15.cloned.1.call-done = bf16[3072,768]{1,0:T(8,128)(2,1)} async-done(((bf16[192,768]{1,0:T(8,128)(2,1)}), bf16[3072,768]{1,0:T(8,128)(2,1)}) %all-gather.15.cloned.1.call-update) | async-done | bytes 4718608 | tf_op jit(solution)/shard_map/all_gather | solution.py:153
  263.2 9.0 convert_reduce_fusion.2
  280.6 8.1 multiply_reduce_fusion.2
  288.7 11.8 %multiply_convert_fusion.1 = bf16[12,400,400]{1,2,0:T(8,128)(2,1)} fusion(f32[12,400,400]{1,2,0:T(8,128)} %get-tuple-element.299, f32[12,400,400]{1,2,0:T(8,128)} %copy-done.1, f32[12,400]{1,0:T(8,128)S(1)} %get-tuple-element.298, f32[12,400]{1,0:T(8,128)S(1)} %log_add_fusion.1), kind=kLoop, calls=%fused_computation.10 | loop fusion | flops 9600000 | bytes 19238400 | tf_op jit(solution)/shard_map/while/body/eval_jaxpr/convert_element_type | solution.py:105
  307.4 6.6 fusion.51
  346.3 5.2 multiply_reduce_fusion.4
  373.1 10.1 multiply_reduce_fusion.1
  383.2 9.1 fusion
  394.6 10.3 fusion.44
  406.4 5.9 fusion.121
  412.3 7.9 convert_reduce_fusion
  438.9 17.5 %multiply_reduce_fusion = (f32[12,576]{1,0:T(8,128)S(1)}, f32[12,576,576]{1,2,0:T(8,128)}) fusion(f32[12,576,576]{1,2,0:T(8,128)} %get-tuple-element.290, f32[12,576]{1,0:T(8,128)S(1)} %log_add_fusion, bf16[576,12,64]{0,2,1:T(8,128)(2,1)} %bitcast.307, bf16[576,12,64]{0,2,1:T(8,128)(2,1)} %bitcast.326), kind=kOutput, calls=%fused_computation.1 | convolution fusion | flops 525526272 | bytes 33675264 | tf_op jit(solution)/shard_map/while/body/eval_jaxpr/qhd,khd->hqk/dot_general | solution.py:101
  456.5 13.4 %multiply_convert_fusion = bf16[12,576,576]{1,2,0:T(8,128)(2,1)S(1)} fusion(f32[12,576,576]{1,2,0:T(8,128)} %get-tuple-element.303, f32[12,576,576]{1,2,0:T(8,128)} %get-tuple-element.290, f32[12,576]{1,0:T(8,128)S(1)} %get-tuple-element.302, f32[12,576]{1,0:T(8,128)S(1)} %log_add_fusion), kind=kLoop, calls=%fused_computation | loop fusion | flops 19906560 | bytes 39868416 | tf_op jit(solution)/shard_map/while/body/eval_jaxpr/convert_element_type | solution.py:105
  469.9 5.2 fusion.114
  481.9 9.4 fusion.45
  501.8 8.6 fusion.118
  514.7 10.3 add_add_fusion.1
  525.5 7.4 multiply_reduce_fusion.7
  551.9 8.0 fusion.88
  559.9 8.1 fusion.72
  568.0 10.4 add_bitcast_fusion
  579.6 5.3 fusion.82
  584.9 7.8 fusion.75
  592.7 8.0 add_add_fusion
  617.9 7.2 convert_bitcast_fusion
  630.5 61.6 %all-reduce.16 = (bf16[768]{0:T(1024)(128)(2,1)S(1)}, bf16[768]{0:T(1024)(128)(2,1)S(1)}, bf16[768]{0:T(1024)(128)(2,1)S(1)}, bf16[768]{0:T(1024)(128)(2,1)S(1)}...) all-reduce(f32[768]{0:T(1024)S(1)} %add_add_fusion.12, ...), channel_id=33, replica_groups=mesh['rep'=2,'fsdp'=16] {'fsdp'}, use_global_device_ids=true, to_apply=%region_38.39.clone | all-reduce | flops 8448 | bytes 50688
  693.5 8.3 copy.182
  701.7 8.8 convert_element_type.497
  710.6 7.8 copy.177
  718.3 5.9 convert_element_type.486
  724.6 8.9 fusion.59
  733.5 5.6 fusion.69
  751.8 74.9 %reduce-scatter.12.cloned.1.call-done = f32[3,1024,48]{1,2,0:T(8,128)} async-done(((f32[3,1024,768]{1,2,0:T(8,128)}), f32[3,1024,48]{1,2,0:T(8,128)}) %reduce-scatter.12.cloned.1.call-update) | async-done | bytes 589840 | tf_op jit(solution)/shard_map/reduce_scatter | solution.py:264
  828.5 113.3 %reduce-scatter.20.cloned.1.call-done = f32[192,768]{1,0:T(8,128)} async-done(((f32[3072,768]{1,0:T(8,128)}), f32[192,768]{1,0:T(8,128)}) %reduce-scatter.20.cloned.1.call-update) | async-done | bytes 589840 | tf_op jit(solution)/shard_map/reduce_scatter | solution.py:218
  943.6 9.8 fusion.56
  953.4 48.2 %reduce-scatter.24.cloned.1.call-done = f32[48,2]{1,0:T(8,128)} async-done(((f32[768,2]{1,0:T(8,128)}), f32[48,2]{1,0:T(8,128)}) %reduce-scatter.24.cloned.1.call-update) | async-done | bytes 400
  1002.3 57.8 %reduce-scatter.22.cloned.1.call-done = f32[48,49]{1,0:T(8,128)} async-done(((f32[768,49]{1,0:T(8,128)}), f32[48,49]{1,0:T(8,128)}) %reduce-scatter.22.cloned.1.call-update) | async-done | bytes 9424
  1061.0 8.3 all-reduce.18
  1074.7 32.7 %all-reduce.22.cloned.1.call-done = (bf16[3,1024,48]{1,2,0:T(8,128)(2,1)}, bf16[48,2304]{1,0:T(8,128)(2,1)}, bf16[48,768]{1,0:T(8,128)(2,1)}, bf16[48,3072]{1,0:T(8,128)(2,1)}, bf16[192,768]{1,0:T(8,128)(2,1)}) async-done(((bf16[3,1024,48]{1,2,0:T(8,128)(2,1)}, bf16[48,2304]{1,0:T(8,128)(2,1)}, bf16[48,768]{1,0:T(8,128)(2,1)}, bf16[48,3072]{1,0:T(8,128)(2,1)}, bf16[192,768]{1,0:T(8,128)(2,1)}), ...) | async-done | bytes 1179664 | tf_op jit(solution)/shard_map/psum | solution.py:336
  (632 shorter events, 245.7 us)
Async XLA Ops:
  7.2 349.9 %copy-start = (f32[256,1024]{1,0:T(8,128)S(1)}, f32[256,1024]{1,0:T(8,128)}, u32[]{:S(2)}) copy-start(f32[256,1024]{1,0:T(8,128)} %param.32) | copy-start | bytes 3145732
  7.2 165.1 %all-gather.7.cloned.1.call-start = ((), (), s32[]{:S(2)}) async-start(), calls=%async_computation.7 | async-start | bytes 5013504 | tf_op jit(solution)/shard_map/all_gather | solution.py:126
  7.9 173.5 %all-gather.9.cloned.1.call-start = ((), (), s32[]{:S(2)}) async-start(), calls=%async_computation.8 | async-start | bytes 3760128 | tf_op jit(solution)/shard_map/all_gather | solution.py:140
  8.7 194.3 %all-gather.11.cloned.1.call-start = ((), (), s32[]{:S(2)}) async-start(), calls=%async_computation.9 | async-start | bytes 1253376 | tf_op jit(solution)/shard_map/all_gather | solution.py:142
  9.4 199.8 %all-gather.13.cloned.1.call-start = ((), (), s32[]{:S(2)}) async-start(), calls=%async_computation.10 | async-start | bytes 5013504 | tf_op jit(solution)/shard_map/all_gather | solution.py:151
  10.0 253.2 %all-gather.15.cloned.1.call-start = ((), (), s32[]{:S(2)}) async-start(), calls=%async_computation.11 | async-start | bytes 5013504 | tf_op jit(solution)/shard_map/all_gather | solution.py:153
  10.6 736.0 %reduce-scatter.16.cloned.1.call-start = ((), (), s32[]{:S(2)}) async-start(), calls=%async_computation.14 | async-start | bytes 2506752 | tf_op jit(solution)/shard_map/reduce_scatter | solution.py:248
  101.0 24.5 %copy-start.106 = (bf16[1,3,240,240]{3,2,1,0:T(8,128)(2,1)S(1)}, bf16[1,3,240,240]{3,2,1,0:T(8,128)(2,1)}, u32[]{:S(2)}) copy-start(bf16[1,3,240,240]{3,2,1,0:T(8,128)(2,1)} %param.28) | copy-start | bytes 1036804
  107.6 73.9 %copy-start.138 = (f32[768]{0:T(1024)}, f32[768]{0:T(1024)S(1)}, u32[]{:S(2)}) copy-start(f32[768]{0:T(1024)S(1)} %convert_element_type.427) | copy-start | bytes 9220
  124.8 78.1 %copy-start.117 = (f32[768]{0:T(1024)}, f32[768]{0:T(1024)S(1)}, u32[]{:S(2)}) copy-start(f32[768]{0:T(1024)S(1)} %convert_element_type.435) | copy-start | bytes 9220
  141.5 38.2 %copy-start.51 = (bf16[400,432]{0,1:T(8,128)(2,1)}, bf16[400,432]{0,1:T(8,128)(2,1)S(1)}, u32[]{:S(2)}) copy-start(bf16[400,432]{0,1:T(8,128)(2,1)S(1)} %reshape.621) | copy-start | bytes 1036804
  141.6 10.7 copy-start.141
  181.1 21.8 %copy-start.9 = (f32[400,768]{1,0:T(8,128)}, f32[400,768]{1,0:T(8,128)S(1)}, u32[]{:S(2)}) copy-start(f32[400,768]{1,0:T(8,128)S(1)} %get-tuple-element.282) | copy-start | bytes 3686404
  205.3 66.9 %copy-start.32 = (f32[400,768]{1,0:T(8,128)}, f32[400,768]{1,0:T(8,128)S(1)}, u32[]{:S(2)}) copy-start(f32[400,768]{1,0:T(8,128)S(1)} %get-tuple-element.286) | copy-start | bytes 3686404
  205.3 69.8 %copy-start.122 = (f32[400]{0:T(512)}, f32[400]{0:T(512)S(1)}, u32[]{:S(2)}) copy-start(f32[400]{0:T(512)S(1)} %broadcast_multiply_fusion.10) | copy-start | bytes 4804
  205.6 69.5 %copy-start.158 = (f32[400]{0:T(512)}, f32[400]{0:T(512)S(1)}, u32[]{:S(2)}) copy-start(f32[400]{0:T(512)S(1)} %add_rsqrt_fusion.2) | copy-start | bytes 4804
  205.7 57.5 %copy-start.102 = (bf16[1,400,768]{2,1,0:T(8,128)(2,1)S(1)}, bf16[1,400,768]{2,1,0:T(8,128)(2,1)}, u32[]{:S(2)}) copy-start(bf16[1,400,768]{2,1,0:T(8,128)(2,1)} %param.52) | copy-start | bytes 1843204
  205.7 57.5 %copy-start.142 = (f32[3072]{0:T(1024)S(1)}, f32[3072]{0:T(1024)}, u32[]{:S(2)}) copy-start(f32[3072]{0:T(1024)} %convert_element_type.439) | copy-start | bytes 36868
  277.7 75.3 %copy-start.7 = (f32[400,768]{1,0:T(8,128)}, f32[400,768]{1,0:T(8,128)S(1)}, u32[]{:S(2)}) copy-start(f32[400,768]{1,0:T(8,128)S(1)} %get-tuple-element.244) | copy-start | bytes 3686404
  288.7 11.8 %copy-start.41 = (bf16[400,768]{0,1:T(8,128)(2,1)S(1)}, bf16[400,768]{0,1:T(8,128)(2,1)}, u32[]{:S(2)}) copy-start(bf16[400,768]{0,1:T(8,128)(2,1)} %copy.161) | copy-start | bytes 1843204
  321.7 10.7 copy-start.5
  331.3 20.2 %copy-start.109 = (f32[12,256]{1,0:T(8,128)}, f32[12,256]{1,0:T(8,128)S(1)}, u32[]{:S(2)}) copy-start(f32[12,256]{1,0:T(8,128)S(1)} %log_add_fusion.2) | copy-start | bytes 36868
  343.9 11.3 %copy-start.26 = (f32[256,768]{1,0:T(8,128)}, f32[256,768]{1,0:T(8,128)S(1)}, u32[]{:S(2)}) copy-start(f32[256,768]{1,0:T(8,128)S(1)} %get-tuple-element.246) | copy-start | bytes 2359300
  363.6 41.3 %copy-start.14 = (f32[576,768]{1,0:T(8,128)}, f32[576,768]{1,0:T(8,128)S(1)}, u32[]{:S(2)}) copy-start(f32[576,768]{1,0:T(8,128)S(1)} %get-tuple-element.288) | copy-start | bytes 5308420
  394.6 10.3 copy-start.13
  394.6 10.3 copy-start.119
  406.0 18.1 %copy-start.17 = (f32[576,768]{1,0:T(8,128)}, f32[576,768]{1,0:T(8,128)S(1)}, u32[]{:S(2)}) copy-start(f32[576,768]{1,0:T(8,128)S(1)} %get-tuple-element.292) | copy-start | bytes 5308420
  406.4 13.8 %slice-start.12 = ((s8[4718592]{0:T(1024)(128)(4,1)}), s8[4194304]{0:T(1024)(128)(4,1)S(1)}, s32[]{:S(2)}) async-start(s8[4718592]{0:T(1024)(128)(4,1)} %bitcast.381), calls=%async_computation.32 | async-start | bytes 8388608
  425.5 9.3 copy-start.22
  436.1 105.5 %copy-start.56 = (bf16[12,64,256]{2,1,0:T(8,128)(2,1)}, bf16[12,64,256]{2,1,0:T(8,128)(2,1)S(1)}, u32[]{:S(2)}) copy-start(bf16[12,64,256]{2,1,0:T(8,128)(2,1)S(1)} %fusion.66) | copy-start | bytes 1179652
  438.9 309.4 %reduce-scatter.14.cloned.1.call-start = ((), (), s32[]{:S(2)}) async-start(), calls=%async_computation.13 | async-start | bytes 7520256 | tf_op jit(solution)/shard_map/reduce_scatter | solution.py:246
  456.4 13.4 %copy-start.10 = (f32[400,768]{1,0:T(8,128)S(1)}, f32[400,768]{1,0:T(8,128)}, u32[]{:S(2)}) copy-start(f32[400,768]{1,0:T(8,128)} %copy-done.9) | copy-start | bytes 3686404
  456.4 13.4 %copy-start.70 = (bf16[12,64,400]{2,1,0:T(8,128)(2,1)S(1)}, bf16[12,64,400]{2,1,0:T(8,128)(2,1)}, u32[]{:S(2)}) copy-start(bf16[12,64,400]{2,1,0:T(8,128)(2,1)} %multiply_convert_fusion.9) | copy-start | bytes 1843204
  456.4 13.4 %copy-start.72 = (bf16[12,64,400]{2,1,0:T(8,128)(2,1)S(1)}, bf16[12,64,400]{2,1,0:T(8,128)(2,1)}, u32[]{:S(2)}) copy-start(bf16[12,64,400]{2,1,0:T(8,128)(2,1)} %multiply_convert_fusion.8) | copy-start | bytes 1843204
  456.4 13.4 %copy-start.74 = (bf16[12,64,400]{2,1,0:T(8,128)(2,1)S(1)}, bf16[12,64,400]{2,1,0:T(8,128)(2,1)}, u32[]{:S(2)}) copy-start(bf16[12,64,400]{2,1,0:T(8,128)(2,1)} %fusion.51) | copy-start | bytes 1843204
  456.4 13.4 %copy-start.121 = (f32[400]{0:T(512)S(1)}, f32[400]{0:T(512)}, u32[]{:S(2)}) copy-start(f32[400]{0:T(512)} %copy-done.120) | copy-start | bytes 4804
  456.4 13.4 %copy-start.140 = (f32[768]{0:T(1024)S(1)}, f32[768]{0:T(1024)}, u32[]{:S(2)}) copy-start(f32[768]{0:T(1024)} %copy-done.138) | copy-start | bytes 9220
  456.5 13.4 %copy-start.157 = (f32[400]{0:T(512)S(1)}, f32[400]{0:T(512)}, u32[]{:S(2)}) copy-start(f32[400]{0:T(512)} %copy-done.156) | copy-start | bytes 4804
  478.2 13.1 %copy-start.45 = (bf16[12,64,576]{2,1,0:T(8,128)(2,1)}, bf16[12,64,576]{2,1,0:T(8,128)(2,1)S(1)}, u32[]{:S(2)}) copy-start(bf16[12,64,576]{2,1,0:T(8,128)(2,1)S(1)} %multiply_convert_fusion.7) | copy-start | bytes 2654212
  481.9 9.5 copy-start.15
  481.9 9.5 copy-start.129
  501.2 248.8 %reduce-scatter.18.cloned.1.call-start = ((), (), s32[]{:S(2)}) async-start(), calls=%async_computation.15 | async-start | bytes 10027008 | tf_op jit(solution)/shard_map/reduce_scatter | solution.py:216
  525.1 301.6 %reduce-scatter.12.cloned.1.call-start = ((), (), s32[]{:S(2)}) async-start(), calls=%async_computation.12 | async-start | bytes 10027008 | tf_op jit(solution)/shard_map/reduce_scatter | solution.py:264
  578.5 363.2 %reduce-scatter.20.cloned.1.call-start = ((), (), s32[]{:S(2)}) async-start(), calls=%async_computation.16 | async-start | bytes 10027008 | tf_op jit(solution)/shard_map/reduce_scatter | solution.py:218
  600.7 400.8 %reduce-scatter.24.cloned.1.call-start = ((), (), s32[]{:S(2)}) async-start(), calls=%async_computation.18 | async-start | bytes 417792
  615.6 444.5 %reduce-scatter.22.cloned.1.call-start = ((), (), s32[]{:S(2)}) async-start(), calls=%async_computation.17 | async-start | bytes 417792
  724.3 383.0 %all-reduce.22.cloned.1.call-start = ((), (), s32[]{:S(2)}) async-start(), calls=%async_computation.19 | async-start | bytes 2359296 | tf_op jit(solution)/shard_map/psum | solution.py:336
  742.4 201.1 %copy-start.19 = (f32[576,768]{1,0:T(8,128)S(1)}, f32[576,768]{1,0:T(8,128)}, u32[]{:S(2)}) copy-start(f32[576,768]{1,0:T(8,128)} %copy-done.17) | copy-start | bytes 5308420
  (161 other events, 712.9 us)
Sparse Core Ops, SparseCore 0:
  10.3 56.6 all-gather.6
  69.3 45.5 all-gather.8
  117.2 37.3 all-gather.10
  156.7 52.4 all-gather.12
  211.4 51.7 all-gather.14
  439.0 61.4 reduce-scatter.15
  505.0 88.9 reduce-scatter.13
  598.2 112.5 reduce-scatter.17
  715.4 111.1 reduce-scatter.11
  830.6 111.0 reduce-scatter.19
  946.2 55.2 reduce-scatter.23
  1005.5 54.6 reduce-scatter.21
  1064.6 42.7 all-reduce.21
where the time goes:
time: 1130 us; the launch traced here: 1120 us
  waiting for transfers between devices  381 us (34%)
  matrix products  325 us (29%)
  blocking collectives  171 us (15%)
  local copies, waits for them, and re-layouts  146 us (13%)
  other arithmetic  78.5 us (7%)
  between operations  19.4 us (2%)
    unnamed x2, blocking collectives  126 us
    reduce_scatter x1, waiting for transfers between devices, run_batch(): lax.psum_scatter(feed_local[4], 'fsdp', scatter_dimension=0, tiled=True)  113 us
    unnamed x15, waiting for transfers between devices  109 us
    reduce_scatter x1, waiting for transfers between devices, run_batch(): lax.psum_scatter(grad_base, 'fsdp', scatter_dimension=2, tiled=True)  74.9 us
    all_gather x1, waiting for transfers between devices, feed_weights(): lax.all_gather(shards[13], 'fsdp', axis=0, tiled=True)  47.2 us
    convert_element_type x6, local copies, waits for them, and re-layouts, run_batch(): unpatch(grad_patches, patch_side, image_count, pixel_side).astype(bf16)  36.4 us
    psum x1, waiting for transfers between devices, body(): lax.psum(shortened(totals), 'rep')  32.7 us
    dot_general x3, matrix products, attend_backward(): jnp.einsum('qhd,khd->hqk', grad_heads, value_rows, preferred_element_type...  30.8 us
  transfers between devices with their start and end apart: 13, of which 7 were waited for; matrix products, arithmetic and copies ran while one was open for 32% of the time, Pallas kernels for 0%

commit v1 on v0

v1 whole, which is shorter than its diff:
```python
import functools
import math

import jax
import jax.numpy as jnp
from jax import lax
from jax.experimental import pallas as pl
from jax.experimental.pallas import tpu as pltpu
from jax.sharding import PartitionSpec as P

HEADS = 12
HEAD = 64
SIDES = (10, 12, 16)
SLOT = 16
F32 = jnp.float32
BF16 = jnp.bfloat16


def swap(value, axis, size, bit):
    return lax.ppermute(value, axis, [(i, i ^ bit) for i in range(size)])


def place_kernel(count, pieces, halves, me_ref, *refs):
    parts, whole, sems = refs[:pieces], refs[pieces], refs[pieces + 1]
    me, other = me_ref[0], me_ref[1]
    copies = []
    for h in range(halves):
        for d in range(count):
            part = parts[(d % 2) * halves + h]
            row = lax.bitwise_xor(me, d)
            if halves == 1:
                target = whole.at[row]
            else:
                width = whole.shape[2] // 2
                start = pl.multiple_of(lax.bitwise_xor(other, h) * width, 128)
                target = whole.at[row, :, pl.ds(start, width)]
            copies.append(pltpu.make_async_copy(part.at[d // 2], target, sems.at[h, d]))
    for copy in copies:
        copy.start()
    for copy in copies:
        copy.wait()


def take_kernel(count, me_ref, whole, keep, give, sems):
    me = me_ref[0]
    copies = []
    for d in range(count):
        target = (keep, give)[d % 2].at[d // 2]
        copies.append(
            pltpu.make_async_copy(whole.at[lax.bitwise_xor(me, d)], target, sems.at[d])
        )
    for copy in copies:
        copy.start()
    for copy in copies:
        copy.wait()


def take(whole, where, count):
    _, rows, columns = whole.shape
    shape = jax.ShapeDtypeStruct((count // 2, rows, columns), whole.dtype)
    return pl.pallas_call(
        functools.partial(take_kernel, count),
        out_shape=(shape, shape),
        in_specs=[pl.BlockSpec(memory_space=pltpu.SMEM), pl.BlockSpec(memory_space=pltpu.VMEM)],
        out_specs=[pl.BlockSpec(memory_space=pl.ANY)] * 2,
        scratch_shapes=[pltpu.SemaphoreType.DMA((count,))],
        compiler_params=pltpu.CompilerParams(vmem_limit_bytes=16 * 2**20),
        cost_estimate=pl.CostEstimate(
            flops=0, bytes_accessed=4 * count * rows * columns, transcendentals=0
        ),
    )(where, whole)


def gather(shard, where, count, split):
    rows, columns = shard.shape
    halves = 2 if split else 1
    if split:
        width = columns // 2
        shard = lax.dynamic_slice_in_dim(shard, where[1] * width, width, 1)
    held = shard[None]
    bit = 2
    steps = []
    while bit < count:
        steps.append(bit)
        bit *= 2
    order = [0]
    for bit in reversed(steps):
        held = jnp.concatenate([held, swap(held, "fsdp", count, bit)])
        order = order + [k ^ (bit // 2) for k in order]
    assert len(order) == count // 2
    near = [held]
    if split:
        near.append(swap(held, "rep", 2, 1))
    far = [swap(part, "fsdp", count, 1) for part in near]
    whole = place(near + far, halves, where, count, order)
    return whole.reshape(count * rows, columns)


def place(parts, halves, where, count, order):
    back = [order.index(k) for k in range(count // 2)]
    _, rows, columns = parts[0].shape

    def kernel(me_ref, *refs):
        named = [Ordered(ref, back) for ref in refs[: len(parts)]]
        place_kernel(count, len(parts), halves, me_ref, *named, *refs[len(parts) :])

    return pl.pallas_call(
        kernel,
        out_shape=jax.ShapeDtypeStruct((count, rows, columns * halves), parts[0].dtype),
        in_specs=[pl.BlockSpec(memory_space=pltpu.SMEM)]
        + [pl.BlockSpec(memory_space=pl.ANY)] * len(parts),
        out_specs=pl.BlockSpec(memory_space=pltpu.VMEM),
        scratch_shapes=[pltpu.SemaphoreType.DMA((halves, count))],
        compiler_params=pltpu.CompilerParams(vmem_limit_bytes=16 * 2**20),
        cost_estimate=pl.CostEstimate(
            flops=0, bytes_accessed=4 * count * rows * columns * halves, transcendentals=0
        ),
    )(where, *parts)


class Ordered:
    def __init__(self, ref, order):
        self.ref, self.order = ref, order
        self.at = self

    def __getitem__(self, k):
        return self.ref.at[self.order[k]]


def add(first, second):
    return (first.astype(F32) + second.astype(F32)).astype(BF16)


def scatter(whole, where, count, split):
    rows, columns = whole.shape[0] // count, whole.shape[1]
    keep, give = take(whole.reshape(count, rows, columns), where, count)
    got = swap(give, "fsdp", count, 1)
    half = columns // 2
    if split:
        mine, theirs = where[1] * half, (1 - where[1]) * half
        cut = lambda part, start: lax.dynamic_slice_in_dim(part, start, half, 2)
        arrived = swap(add(cut(keep, theirs), cut(got, theirs)), "rep", 2, 1)
        held = add3(cut(keep, mine), cut(got, mine), arrived)
    else:
        held = None
    size, bit = count // 4, 2
    while size:
        if held is None:
            pairs_k = keep.reshape(size, 2, rows, columns)
            pairs_g = got.reshape(size, 2, rows, columns)
            there = add(pairs_k[:, 1], pairs_g[:, 1])
            here = add(pairs_k[:, 0], pairs_g[:, 0])
        else:
            pairs = held.reshape(size, 2, rows, held.shape[2])
            there, here = pairs[:, 1], pairs[:, 0]
        held = add(here, swap(there, "fsdp", count, bit))
        size, bit = size // 2, bit * 2
    held = held[0]
    if split:
        other = swap(held, "rep", 2, 1)
        low = where[1] == 0
        return jnp.concatenate(
            [jnp.where(low, held, other), jnp.where(low, other, held)], axis=1
        ).astype(F32)
    return add(held, swap(held, "rep", 2, 1)).astype(F32)


def add3(first, second, third):
    return (first.astype(F32) + second.astype(F32) + third.astype(F32)).astype(BF16)


def up_to(value, unit):
    return -(-value // unit) * unit

def swap_chunks(lines):
    chunk = lax.broadcasted_iota(jnp.int32, lines[0].shape, 1) // SLOT
    for step in (1, 2, 4):
        stays = (chunk & step) == 0
        for i in range(8):
            if i & step == 0:
                low, high = lines[i], lines[i + step]
                lines[i] = jnp.where(stays, low, pltpu.roll(high, step * SLOT, 1))
                lines[i + step] = jnp.where(stays, pltpu.roll(low, 128 - step * SLOT, 1), high)
    return lines

def spread(side, grid, columns):
    pixel = lax.broadcasted_iota(jnp.int32, (grid * side, columns), 0)
    column = lax.broadcasted_iota(jnp.int32, (grid * side, columns), 1)
    place = column % SLOT
    return ((pixel == column // SLOT * side + place) & (place < side)).astype(BF16)

def patch_kernel(*refs):
    pixels, outs, rows_ref, flat_ref = refs[:3], refs[3:6], refs[6], refs[7]
    for side, pixel_ref, out in zip(SIDES, pixels, outs):
        high = pixel_ref.shape[2]
        grid = high // side
        columns = up_to(grid * SLOT, 128)
        table = None if side == SLOT else spread(side, grid, columns)
        for c in range(3):
            picture = pixel_ref[0, c]
            if table is None:
                wide = picture.astype(F32)
            else:
                wide = jnp.dot(picture, table, preferred_element_type=F32)
            for block in range(columns // 128):
                rows_ref[3 * c + block, :high, :] = wide[:, 128 * block:128 * block + 128]
        slots = 3 * side
        for group in range(out.shape[1] // 128):
            for block in range(columns // 128):
                lines = []
                for q in range(8 * group, 8 * group + 8):
                    if q < slots:
                        lines.append(rows_ref[q // side * 3 + block, pl.ds(q % side, grid, stride=side), :])
                    else:
                        lines.append(jnp.zeros((grid, 128), F32))
                lines = swap_chunks(lines)
                for g in range(8):
                    if 8 * block + g < grid:
                        flat_ref[group, pl.ds(8 * block + g, grid, stride=grid), :] = lines[g]
        for group in range(out.shape[1] // 128):
            out[:, 128 * group:128 * group + 128] = flat_ref[group, :grid * grid, :].astype(BF16)

def patch_all(pixels):
    shapes = []
    for picture, side in zip(pixels, SIDES):
        grid = picture.shape[2] // side
        shapes.append(jax.ShapeDtypeStruct((grid * grid, up_to(3 * side * SLOT, 128)), BF16))
    high = max(p.shape[2] for p in pixels)
    return pl.pallas_call(
        patch_kernel,
        out_shape=shapes,
        in_specs=[pl.BlockSpec(memory_space=pltpu.VMEM)] * 3,
        out_specs=[pl.BlockSpec(memory_space=pltpu.VMEM)] * 3,
        scratch_shapes=[pltpu.VMEM((9, high, 128), F32), pltpu.VMEM((max(s.shape[1] for s in shapes) // 128, max(s.shape[0] for s in shapes), 128), F32)],
        compiler_params=pltpu.CompilerParams(vmem_limit_bytes=24 * 2**20),
        cost_estimate=pl.CostEstimate(flops=5 * 10**9, bytes_accessed=4 * 10**6, transcendentals=0),
    )(*pixels)

def unpatch_kernel(starts, bounds, grad_ref, kernel_ref, *refs):
    outs, flat_ref, rows_ref = refs[:3], refs[3], refs[4]
    for i, side in enumerate(SIDES):
        out = outs[i]
        high = out.shape[2]
        grid = high // side
        columns = up_to(grid * SLOT, 128)
        width = bounds[i + 1] - bounds[i]
        grads = grad_ref[starts[i]:starts[i + 1], :]
        flat = jnp.dot(grads, kernel_ref[:, bounds[i]:bounds[i + 1]], preferred_element_type=F32)
        for group in range(width // 128):
            flat_ref[group, :grid * grid, :] = flat[:, 128 * group:128 * group + 128]
        slots = 3 * side
        for group in range(width // 128):
            for block in range(columns // 128):
                lines = []
                for g in range(8):
                    if 8 * block + g < grid:
                        lines.append(flat_ref[group, pl.ds(8 * block + g, grid, stride=grid), :])
                    else:
                        lines.append(jnp.zeros((grid, 128), F32))
                lines = swap_chunks(lines)
                for q in range(8 * group, min(8 * group + 8, slots)):
                    rows_ref[q // side * 3 + block, pl.ds(q % side, grid, stride=side), :] = lines[q % 8]
        table = None if side == SLOT else spread(side, grid, columns)
        for c in range(3):
            picture = jnp.concatenate([rows_ref[3 * c + block, :high, :] for block in range(columns // 128)], axis=1).astype(BF16)
            if table is not None:
                picture = lax.dot_general(picture, table, (((1,), (1,)), ((), ())), preferred_element_type=F32).astype(BF16)
            out[0, c] = picture

def unpatch_all(grads, kernels, starts, bounds, sides):
    high = max(sides)
    whole = pl.BlockSpec(memory_space=pltpu.VMEM)
    return pl.pallas_call(
        functools.partial(unpatch_kernel, starts, bounds),
        out_shape=[jax.ShapeDtypeStruct((1, 3, s, s), BF16) for s in sides],
        in_specs=[whole] * 2,
        out_specs=[whole] * 3,
        scratch_shapes=[pltpu.VMEM((max(e - s for s, e in zip(bounds, bounds[1:])) // 128, max(e - s for s, e in zip(starts, starts[1:])), 128), F32),
            pltpu.VMEM((9, high, 128), F32)],
        compiler_params=pltpu.CompilerParams(vmem_limit_bytes=32 * 2**20),
        cost_estimate=pl.CostEstimate(flops=5 * 10**9, bytes_accessed=10 * 10**6, transcendentals=0),
    )(grads, kernels)


def three_terms(value):
    first = lax.reduce_precision(value, 8, 7)
    rest = value - first
    second = lax.reduce_precision(rest, 8, 7)
    return first.astype(BF16), second.astype(BF16), (rest - second).astype(BF16)


def exact_dot(value, low, dims):
    return sum(
        lax.dot_general(term, low, dims, preferred_element_type=F32)
        for term in reversed(three_terms(value))
    )


def unit(values):
    mean_row = jnp.mean(values, axis=-1, keepdims=True)
    centred = values - mean_row
    inverse = lax.rsqrt(jnp.mean(centred * centred, axis=-1, keepdims=True) + 1e-06)
    return centred * inverse, inverse


def norm_backward(grad_out, unit_rows, inverse, gain):
    grad_unit = grad_out * gain
    inner = jnp.mean(grad_unit * unit_rows, axis=-1, keepdims=True)
    grad_in = inverse * (
        grad_unit - jnp.mean(grad_unit, axis=-1, keepdims=True) - unit_rows * inner
    )
    return grad_in, jnp.sum(grad_out * unit_rows, axis=0), jnp.sum(grad_out, axis=0)


def chunks(total, most):
    pieces = -(-total // most)
    size = -(-total // pieces)
    size = -(-size // 16) * 16
    return [(s, min(size, total - s)) for s in range(0, total, size)]

def outer_t(first, second):
    return lax.dot_general(first, second, (((1,), (1,)), ((), ())), preferred_element_type=F32)

def attend_kernel(starts, chunk, q_ref, k_ref, v_ref, mixed_ref, total_ref):
    pair = pl.program_id(0)
    @pl.when(pair == 0)
    def _():
        total_ref[...] = jnp.zeros_like(total_ref)
    for begin, end in zip(starts, starts[1:]):
        keys, values = k_ref[begin:end, :], v_ref[begin:end, :]
        for offset, size in chunks(end - begin, chunk):
            rows = slice(begin + offset, begin + offset + size)
            queries = q_ref[rows, :] * (HEAD ** -0.5)
            lane = lax.broadcasted_iota(jnp.int32, (size, 128), 1)
            mixed, totals = [], []
            for head in range(2):
                own = (lane < HEAD) if head == 0 else (lane >= HEAD)
                scores = outer_t(jnp.where(own, queries, jnp.zeros_like(queries)), keys)
                top = jnp.max(scores, axis=1, keepdims=True)
                expo = jnp.exp(scores - top)
                total = jnp.sum(expo, axis=1, keepdims=True)
                out = jnp.dot(expo.astype(BF16), values, preferred_element_type=F32)
                mixed.append(out / total)
                totals.append(top + jnp.log(total))
            mixed_ref[rows, :] = jnp.where(lane < HEAD, mixed[0], mixed[1]).astype(BF16)
            held = total_ref[rows, :]
            held = jnp.where(lane == 2 * pair, totals[0], held)
            total_ref[rows, :] = jnp.where(lane == 2 * pair + 1, totals[1], held)

def attend_forward(qkv, starts, chunk=576):
    rows, width = qkv.shape[0], qkv.shape[1] // 3
    pairs = width // 128
    block = lambda first: pl.BlockSpec((rows, 128), lambda j: (0, first * pairs + j))
    return pl.pallas_call(
        functools.partial(attend_kernel, starts, chunk),
        grid=(pairs,),
        out_shape=(jax.ShapeDtypeStruct((rows, width), BF16), jax.ShapeDtypeStruct((rows, 128), F32)),
        in_specs=[block(0), block(1), block(2)],
        out_specs=[pl.BlockSpec((rows, 128), lambda j: (0, j)), pl.BlockSpec((rows, 128), lambda j: (0, 0))],
        compiler_params=pltpu.CompilerParams(vmem_limit_bytes=32 * 2**20),
        cost_estimate=pl.CostEstimate(flops=20 * 10**9, bytes_accessed=8 * rows * width, transcendentals=0),
    )(qkv, qkv, qkv)

def terms(value):
    first = value.astype(BF16)
    rest = value - first.astype(F32)
    second = rest.astype(BF16)
    return first, second, (rest - second.astype(F32)).astype(BF16)

def attend_back_kernel(starts, chunk, q_ref, k_ref, v_ref, mixed_ref, grad_ref, total_ref, out_ref, left, right, acc):
    pair = pl.program_id(0)
    scale = HEAD ** -0.5
    zero = jnp.zeros((), BF16)
    for begin, end in zip(starts, starts[1:]):
        size = end - begin
        for offset, part in chunks(size, chunk):
            rows = slice(begin + offset, begin + offset + part)
            lane = lax.broadcasted_iota(jnp.int32, (part, 128), 1)
            queries, grads = q_ref[rows, :] * scale, grad_ref[rows, :]
            product = grads.astype(F32) * mixed_ref[rows, :].astype(F32)
            total_all = total_ref[rows, :]
            for head in range(2):
                own = (lane < HEAD) if head == 0 else (lane >= HEAD)
                free = HEAD * (1 - head)
                inner = jnp.sum(jnp.where(own, product, 0.0), axis=1, keepdims=True)
                total = jnp.sum(jnp.where(lane == 2 * pair + head, total_all, 0.0), axis=1, keepdims=True)
                for target, value, line in ((left, queries, total), (right, grads, inner)):
                    wide = jnp.where(own, value, zero)
                    for i, term in enumerate(terms(line)):
                        wide = jnp.where(lane == free + i, term, wide)
                    target[head, offset:offset + part, :] = wide
        queries, grads = q_ref[begin:end, :], grad_ref[begin:end, :]
        acc[...] = jnp.zeros_like(acc)
        for offset, part in chunks(size, chunk):
            rows = slice(begin + offset, begin + offset + part)
            lane = lax.broadcasted_iota(jnp.int32, (part, 128), 1)
            keys, values = k_ref[rows, :], v_ref[rows, :]
            grad_key, grad_value = [], []
            for head in range(2):
                own = (lane < HEAD) if head == 0 else (lane >= HEAD)
                free = HEAD * (1 - head)
                minus = jnp.where((lane >= free) & (lane < free + 3), -jnp.ones((), BF16), zero)
                scores = outer_t(jnp.where(own, keys, minus), left[head, :size, :])
                probs = jnp.exp(scores)
                grad_scores = outer_t(jnp.where(own, values, minus), right[head, :size, :])
                grad_scores = (probs * grad_scores).astype(BF16)
                grad_value.append(jnp.dot(probs.astype(BF16), grads, preferred_element_type=F32))
                grad_key.append(jnp.dot(grad_scores, queries, preferred_element_type=F32))
                acc[head, :size, :] += lax.dot_general(grad_scores, keys, (((0,), (0,)), ((), ())), preferred_element_type=F32)
            out_ref[1, rows, :] = (jnp.where(lane < HEAD, *grad_key) * scale).astype(BF16)
            out_ref[2, rows, :] = jnp.where(lane < HEAD, *grad_value).astype(BF16)
        lane = lax.broadcasted_iota(jnp.int32, (size, 128), 1)
        out_ref[0, begin:end, :] = (jnp.where(lane < HEAD, acc[0, :size, :], acc[1, :size, :]) * scale).astype(BF16)

def attend_backward(qkv, mixed, totals, grad_mixed, starts, chunk=400):
    rows, width = mixed.shape
    pairs = width // 128
    longest = max(e - s for s, e in zip(starts, starts[1:]))
    block = lambda first: pl.BlockSpec((rows, 128), lambda j: (0, first * pairs + j))
    return pl.pallas_call(
        functools.partial(attend_back_kernel, starts, chunk),
        grid=(pairs,),
        out_shape=jax.ShapeDtypeStruct((3, rows, width), BF16),
        in_specs=[block(0), block(1), block(2), block(0), block(0), pl.BlockSpec((rows, 128), lambda j: (0, 0))],
        out_specs=pl.BlockSpec((3, rows, 128), lambda j: (0, 0, j)),
        scratch_shapes=[pltpu.VMEM((2, longest, 128), BF16), pltpu.VMEM((2, longest, 128), BF16), pltpu.VMEM((2, longest, 128), F32)],
        compiler_params=pltpu.CompilerParams(vmem_limit_bytes=32 * 2**20),
        cost_estimate=pl.CostEstimate(flops=40 * 10**9, bytes_accessed=16 * rows * width, transcendentals=0),
    )(qkv, qkv, qkv, mixed, grad_mixed, totals)


def dot(first, second):
    return jnp.dot(first, second, preferred_element_type=F32)


def dot_t(first, second):
    return lax.dot_general(first, second, (((1,), (1,)), ((), ())), preferred_element_type=F32)


def t_dot(first, second):
    return lax.dot_general(first, second, (((0,), (0,)), ((), ())), preferred_element_type=F32)


def body(count, pixels, resizes, posmaps, weights, cotangents):
    base_kernel, patch_bias, posemb = weights[:3]
    ln1_gain, ln1_bias, qkv_weight, qv_bias, out_weight, out_bias = weights[3:9]
    ln2_gain, ln2_bias, up_weight, up_bias, down_weight, down_bias = weights[9:]
    channels, base_pixels, share = base_kernel.shape
    width = share * count
    spots = posemb.shape[0]
    where = jnp.stack([lax.axis_index("fsdp"), lax.axis_index("rep")]).astype(jnp.int32)
    tokens = [c.shape[1] for c in cotangents]
    starts = [sum(tokens[:i]) for i in range(4)]
    part = lambda rows, i: rows[starts[i] : starts[i + 1]]

    padded = []
    for resize, side in zip(resizes, SIDES):
        wide = jnp.pad(
            resize.reshape(side, side, base_pixels), ((0, 0), (0, SLOT - side), (0, 0))
        )
        padded.append(wide.reshape(side * SLOT, base_pixels))
    resize_all = jnp.concatenate(padded)
    pixel_rows = resize_all.shape[0]
    bounds = [0]
    for side in SIDES:
        bounds.append(bounds[-1] + side * SLOT)
    base_rows = base_kernel.transpose(1, 0, 2).reshape(base_pixels, channels * share)
    resized = exact_dot(resize_all, base_rows, (((1,), (0,)), ((), ()))).astype(BF16)
    resized = resized.reshape(pixel_rows, channels, share).transpose(2, 1, 0)
    kernel_shard, kernel_bounds = [], [0]
    for i, side in enumerate(SIDES):
        columns = up_to(3 * side * SLOT, 128)
        own = resized[:, :, bounds[i] : bounds[i + 1]].reshape(share, -1)
        kernel_shard.append(jnp.pad(own, ((0, 0), (0, columns - own.shape[1]))))
        kernel_bounds.append(kernel_bounds[-1] + columns)
    kernel_shard = jnp.concatenate(kernel_shard, axis=1)
    up_per = up_bias.shape[0] // share
    smalls = [posemb.T] + [
        v.reshape(share, 1)
        for v in (
            patch_bias,
            ln1_gain,
            ln1_bias,
            qv_bias[0],
            qv_bias[1],
            out_bias,
            ln2_gain,
            ln2_bias,
            down_bias,
        )
    ]
    smalls.append(up_bias.reshape(share, up_per))
    used = spots + 9 + up_per
    kernel_columns = kernel_shard.shape[1]
    tail = (-(kernel_columns + used)) % 256
    smalls.append(jnp.zeros((share, tail), BF16))
    embed_shard = jnp.concatenate([kernel_shard] + smalls, axis=1)

    embed_whole = gather(embed_shard, where, count, True)
    w_qkv = gather(qkv_weight, where, count, True)
    w_out = gather(out_weight, where, count, True)
    w_up = gather(up_weight, where, count, True)
    w_down = gather(down_weight, where, count, False)

    kernels = [embed_whole[:, kernel_bounds[i] : kernel_bounds[i + 1]] for i in range(3)]
    table = embed_whole[:, kernel_columns : kernel_columns + used].astype(F32)
    pos_table = table[:, :spots]
    lines = table[:, spots : spots + 9].T
    b_up = table[:, spots + 9 :].reshape(-1)

    patches = patch_all(pixels)
    positions = exact_dot(
        jnp.concatenate(posmaps), pos_table.astype(BF16), (((1,), (1,)), ((), ()))
    )
    embedded = (
        jnp.concatenate([dot_t(p, k) for p, k in zip(patches, kernels)]) + lines[0] + positions
    )
    unit_in, inverse_in = unit(embedded)
    normed_in = (unit_in * lines[1] + lines[2]).astype(BF16)
    bias_three = jnp.concatenate([lines[3], jnp.zeros_like(lines[3]), lines[4]])
    qkv = (dot(normed_in, w_qkv) + bias_three).astype(BF16)
    mixed, totals = attend_forward(qkv, starts)
    middle = embedded + dot(mixed, w_out) + lines[5]
    unit_mid, inverse_mid = unit(middle)
    normed_mid = (unit_mid * lines[6] + lines[7]).astype(BF16)
    up_pre = dot(normed_mid, w_up) + b_up
    act, gelu_back = jax.vjp(jax.nn.gelu, up_pre)
    act = act.astype(BF16)
    final = (middle + dot(act, w_down) + lines[8]).astype(BF16)

    grad_down = jnp.concatenate([c[0] for c in cotangents])
    grad_final = grad_down.astype(F32)
    grad_w_down = t_dot(act, grad_down).astype(BF16)
    sum_down = scatter(grad_w_down, where, count, False)
    grad_up = gelu_back(dot_t(grad_down, w_down))[0].astype(BF16)
    grad_w_up = t_dot(normed_mid, grad_up).astype(BF16)
    sum_up = scatter(grad_w_up, where, count, True)
    grad_normed_mid = dot_t(grad_up, w_up)
    grad_mid, grad_gain2, grad_bias2 = norm_backward(
        grad_normed_mid, unit_mid, inverse_mid, lines[6]
    )
    grad_middle = grad_final + grad_mid
    grad_branch = grad_middle.astype(BF16)
    grad_w_out = t_dot(mixed, grad_branch).astype(BF16)
    grad_mixed = dot_t(grad_branch, w_out).astype(BF16)
    grad_qkv = attend_backward(qkv, mixed, totals, grad_mixed, starts)
    grad_w_qkv = [t_dot(normed_in, grad_qkv[i]).astype(BF16) for i in range(3)]
    sum_attn = scatter(
        jnp.concatenate(grad_w_qkv + [grad_w_out], axis=1), where, count, True
    )
    grad_normed_in = sum(
        dot_t(grad_qkv[i], w_qkv[:, i * width : (i + 1) * width]) for i in range(3)
    )
    grad_in, grad_gain1, grad_bias1 = norm_backward(
        grad_normed_in, unit_in, inverse_in, lines[1]
    )
    grad_embedded = grad_middle + grad_in
    grad_low = grad_embedded.astype(BF16)
    grad_kernel = [t_dot(part(grad_low, i), patches[i]) for i in range(3)]
    grad_table = lax.dot_general(
        grad_embedded,
        jnp.concatenate(posmaps),
        (((0,), (0,)), ((), ())),
        precision=lax.Precision.HIGHEST,
    )
    column_sums = [jnp.sum(grad_qkv[i].astype(F32), axis=0) for i in (0, 2)]
    grad_lines = jnp.stack(
        [
            jnp.sum(grad_embedded, axis=0),
            grad_gain1,
            grad_bias1,
            column_sums[0],
            column_sums[1],
            jnp.sum(grad_branch.astype(F32), axis=0),
            grad_gain2,
            grad_bias2,
            jnp.sum(grad_final, axis=0),
        ]
    )
    grad_b_up = jnp.sum(grad_up.astype(F32), axis=0).reshape(width, up_per)
    grad_embed = jnp.concatenate(
        grad_kernel + [grad_table, grad_lines.T, grad_b_up, jnp.zeros((width, tail), F32)], axis=1
    ).astype(BF16)
    sum_embed = scatter(grad_embed, where, count, True)
    pixel_grads = unpatch_all(
        grad_low, embed_whole, starts, kernel_bounds, [p.shape[2] for p in pixels]
    )

    kernel_sum = jnp.concatenate(
        [
            sum_embed[:, start : start + channels * side * SLOT].reshape(share, channels, -1)
            for start, side in zip(kernel_bounds, SIDES)
        ],
        axis=2,
    )
    base_grad = exact_dot(
        resize_all, kernel_sum.astype(BF16).transpose(2, 1, 0).reshape(pixel_rows, -1),
        (((0,), (0,)), ((), ())),
    )
    base_grad = base_grad.reshape(base_pixels, channels, share).transpose(1, 0, 2)
    small_sum = sum_embed[:, kernel_columns : kernel_columns + used]
    columns = small_sum[:, spots : spots + 9].T
    results = [part(final, i)[None] for i in range(3)]
    return (
        *results,
        *pixel_grads,
        base_grad,
        columns[0],
        small_sum[:, :spots].T,
        columns[1],
        columns[2],
        sum_attn[:, : 3 * width],
        columns[3:5],
        sum_attn[:, 3 * width :],
        columns[5],
        columns[6],
        columns[7],
        sum_up,
        small_sum[:, spots + 9 :].reshape(-1),
        sum_down,
        columns[8],
    )


def solution(mesh):
    count = mesh.shape["fsdp"]

    def run(*args):
        return body(count, args[:3], args[3:6], args[6:9], args[9:24], args[24:])

    images = ("rep", "fsdp")
    weight_specs = (
        P(None, None, "fsdp"),
        P("fsdp"),
        P(None, "fsdp"),
        P("fsdp"),
        P("fsdp"),
        P("fsdp", None),
        P(None, "fsdp"),
        P("fsdp", None),
        P("fsdp"),
        P("fsdp"),
        P("fsdp"),
        P("fsdp", None),
        P("fsdp"),
        P("fsdp", None),
        P("fsdp"),
    )
    return jax.shard_map(
        run,
        mesh=mesh,
        in_specs=(P(images, None, None, None),) * 3
        + (P(),) * 6
        + weight_specs
        + (P(images, None, None),) * 3,
        out_specs=(P(images, None, None),) * 3
        + (P(images, None, None, None),) * 3
        + weight_specs,
        check_vma=False,
    )
```

time: 1130 us -> 544 us (0.48)
  waiting for transfers between devices: 381 us -> 141 us
  matrix products: 325 us -> 137 us
  blocking collectives: 171 us -> 0 us
  local copies, waits for them, and re-layouts: 146 us -> 60.5 us
  Pallas kernels: 0 us -> 82.6 us
  starting transfers between devices: 1.5 us -> 58.3 us
  other arithmetic: 78.5 us -> 52.3 us
  between operations: 19.4 us -> 2.75 us
    dot_general x75 -> x32, matrix products: 325 us -> 137 us  [the longest x9 49.1 us: dot_t(): lax.dot_general(first, second, (((1,), (1,)), ((), ())), preferred_elemen...]
    reduce_scatter x5 -> x0, waiting for transfers between devices: 188 us -> none  [the longest x1 113 us: run_batch(): lax.psum_scatter(feed_local[4], 'fsdp', scatter_dimension=0, tiled=True)]
    ppermute x0 -> x51, waiting for transfers between devices: none -> 141 us  [swap(): return lax.ppermute(value, axis, [(i, i ^ bit) for i in range(size)])]
    unnamed x2 -> x0, blocking collectives: 126 us -> none
    unnamed x15 -> x0, waiting for transfers between devices: 109 us -> none
    pallas_call x0 -> x13, Pallas kernels: none -> 82.6 us  [the longest x1 28.4 us: attend_backward(): pl.pallas_call(functools.partial(attend_back_kernel, starts, chunk), grid...]
    ppermute x0 -> x51, starting transfers between devices: none -> 58.3 us  [swap(): return lax.ppermute(value, axis, [(i, i ^ bit) for i in range(size)])]
    all_gather x5 -> x0, waiting for transfers between devices: 50.8 us -> none  [the longest x1 47.2 us: feed_weights(): lax.all_gather(shards[13], 'fsdp', axis=0, tiled=True)]
  transfers between devices with their start and end apart: 13 -> 51, of which waited for: 7 -> 20; matrix products, arithmetic and copies ran while one was open for 32% -> 43% of each run, Pallas kernels for 0% -> 15%
where the time goes in v1:
time: 544 us; the launch traced here: 535 us
  waiting for transfers between devices  141 us (26%)
  matrix products  137 us (25%)
  Pallas kernels  82.6 us (15%)
  local copies, waits for them, and re-layouts  60.5 us (11%)
  starting transfers between devices  58.3 us (11%)
  other arithmetic  52.3 us (10%)
    ppermute x51, waiting for transfers between devices, swap(): return lax.ppermute(value, axis, [(i, i ^ bit) for i in range(size)])  141 us
    ppermute x51, starting transfers between devices, swap(): return lax.ppermute(value, axis, [(i, i ^ bit) for i in range(size)])  58.3 us
    dot_general x9, matrix products, dot_t(): lax.dot_general(first, second, (((1,), (1,)), ((), ())), preferred_elemen...  49.1 us
    dot_general x9, matrix products, t_dot(): lax.dot_general(first, second, (((0,), (0,)), ((), ())), preferred_elemen...  39.4 us
    dot_general x4, matrix products, dot(): return jnp.dot(first, second, preferred_element_type=F32)  30.3 us
    pallas_call x1, Pallas kernels, attend_backward(): pl.pallas_call(functools.partial(attend_back_kernel, starts, chunk), grid...  28.4 us
    concatenate x15, other arithmetic, gather(): held = jnp.concatenate([held, swap(held, 'fsdp', count, bit)])  20.5 us
    pallas_call x1, Pallas kernels, attend_forward(): pl.pallas_call(functools.partial(attend_kernel, starts, chunk), grid=(pai...  18.6 us
  transfers between devices with their start and end apart: 51, of which 20 were waited for; matrix products, arithmetic and copies ran while one was open for 43% of the time, Pallas kernels for 15%

profile of v1, /device:TPU:0, one launch (start us, length us, event | category | flops | bytes accessed | tf_op | source)
XLA Modules:
  0.0 534.9 jit_solution(7780476020922906054)
XLA Ops:
  1.5 4.0 collective-permute-start.12
  7.5 3.0 collective-permute-start.18
  18.9 2.9 collective-permute-start
  24.3 13.3 %collective-permute-done = bf16[1,48,1024]{2,1,0:T(8,128)(2,1)S(1)} collective-permute-done((bf16[1,48,1024]{2,1,0:T(8,128)(2,1)S(1)}, bf16[1,48,1024]{2,1,0:T(8,128)(2,1)S(1)}, u32[]{:S(2)}, u32[]{:S(2)}) %collective-permute-start) | collective-permute-done | bytes 98336 | tf_op jit(solution)/shard_map/ppermute | solution.py:20
  59.1 3.6 collective-permute-done.15.refs_1_
  76.3 6.5 %collective-permute-done.8 = bf16[4,48,1152]{2,1,0:T(8,128)(2,1)S(1)} collective-permute-done((bf16[4,48,1152]{2,1,0:T(8,128)(2,1)S(1)}, bf16[4,48,1152]{2,1,0:T(8,128)(2,1)S(1)}, u32[]{:S(2)}, u32[]{:S(2)}) %collective-permute-start.8) | collective-permute-done | bytes 442400 | tf_op jit(solution)/shard_map/ppermute | solution.py:20
  92.0 6.8 %shard_map.418 = (bf16[256,512]{1,0:T(8,128)(2,1)S(1)}, bf16[400,640]{1,0:T(8,128)(2,1)S(1)}, bf16[576,768]{1,0:T(8,128)(2,1)S(1)}) custom-call(bf16[1,3,160,160]{3,2,1,0:T(8,128)(2,1)S(1)} %copy-done.29, bf16[1,3,240,240]{3,2,1,0:T(8,128)(2,1)S(1)} %copy-done.28, bf16[1,3,384,384]{3,2,1,0:T(8,128)(2,1)S(1)} %copy-done.27), custom_call_target="tpu_custom_call" | custom-call | flops 5000000000 | bytes 4000000 | tf_op jit(solution)/shard_map/pallas_call | solution.py:229
  101.3 3.4 collective-permute-done.26
  104.7 3.1 pad_maximum_fusion.2.refs_0_
  108.2 20.9 %collective-permute-done.9.refs_1_ = bf16[8,48,1152]{2,1,0:T(8,128)(2,1)} collective-permute-done((bf16[8,48,1152]{2,1,0:T(8,128)(2,1)}, bf16[8,48,1152]{2,1,0:T(8,128)(2,1)}, u32[]{:S(2)}, u32[]{:S(2)}) %collective-permute-start.9) | collective-permute-done | bytes 884768 | tf_op jit(solution)/shard_map/ppermute | solution.py:20
  139.8 5.2 slice_reduce_fusion.4
  151.6 3.0 shard_map.420
  156.3 4.9 fusion.7.q_ref.k_ref.v_ref
  161.2 18.6 %shard_map.421 = (bf16[1232,768]{1,0:T(8,128)(2,1)S(1)}, f32[1232,128]{1,0:T(8,128)S(1)}) custom-call(bf16[1232,2304]{1,0:T(8,128)(2,1)S(1)} %fusion.7.q_ref.k_ref.v_ref, bf16[1232,2304]{1,0:T(8,128)(2,1)S(1)} %fusion.7.q_ref.k_ref.v_ref, bf16[1232,2304]{1,0:T(8,128)(2,1)S(1)} %fusion.7.q_ref.k_ref.v_ref), custom_call_target="tpu_custom_call" | custom-call | flops 20000000000 | bytes 7569408 | tf_op jit(solution)/shard_map/pallas_call | solution.py:354
  182.4 3.3 shard_map.423
  185.8 9.9 %fusion.82 = f32[1232,3072]{1,0:T(8,128)} fusion(bf16[768,3072]{1,0:T(8,128)(2,1)S(1)} %bitcast.287, f32[1232,768]{1,0:T(8,128)S(1)} %get-tuple-element.157, f32[768]{0:T(1024)S(1)} %get-tuple-element.128, f32[768]{0:T(1024)S(1)} %get-tuple-element.126, f32[1232]{0:T(1024)S(1)} %add_rsqrt_fusion, f32[1232]{0:T(1024)S(1)} %broadcast_multiply_fusion.4), kind=kOutput, calls=%fused_computation.243 | convolution fusion | flops 5818036224 | bytes 23658112 | tf_op jit(solution)/shard_map/dot_general | solution.py:433
  195.6 12.3 %convolution_convert_fusion = bf16[3072,768]{1,0:T(8,128)(2,1)S(1)} fusion(bf16[576,768]{1,0:T(8,128)(2,1)S(1)} %bitcast.304, bf16[400,768]{1,0:T(8,128)(2,1)S(1)} %bitcast.324, bf16[256,768]{1,0:T(8,128)(2,1)S(1)} %bitcast.330, f32[1232,3072]{1,0:T(8,128)} %fusion.82, f32[3072]{0:T(1024)S(1)} %add.266), kind=kOutput, calls=%fused_computation.12 | convolution fusion | flops 5859188736 | bytes 21762048 | tf_op jit(solution)/shard_map/dot_general | solution.py:441
  212.0 3.0 shard_map.424
  215.0 20.7 %fusion.86 = (bf16[3072]{0:T(1024)(128)(2,1)S(1)}, bf16[1232,3072]{1,0:T(8,128)(2,1)}) fusion(f32[1232,3072]{1,0:T(8,128)} %fusion.82, f32[3072]{0:T(1024)S(1)} %add.266, bf16[3072,768]{1,0:T(8,128)(2,1)S(1)} %bitcast.285, bf16[576,768]{1,0:T(8,128)(2,1)} %bitcast.303, bf16[400,768]{1,0:T(8,128)(2,1)} %bitcast.323, bf16[256,768]{1,0:T(8,128)(2,1)S(1)} %bitcast.331), kind=kOutput, calls=%fused_computation.247 | convolution fusion | flops 5902242816 | bytes 29337600 | tf_op jit(solution)/shard_map/dot_general | solution.py:437
  235.7 11.8 %multiply_reduce_fusion = (bf16[768]{0:T(1024)(128)(2,1)S(1)}, f32[1232]{0:T(1024)S(1)}, f32[1232]{0:T(1024)S(1)}, bf16[768]{0:T(1024)(128)(2,1)S(1)}, f32[1232,768]{1,0:T(8,128)S(1)}) fusion(f32[1232,768]{1,0:T(8,128)} %copy-done.42, f32[1232]{0:T(1024)S(1)} %add_rsqrt_fusion, f32[1232]{0:T(1024)S(1)} %broadcast_multiply_fusion.4, ...), kind=kOutput, calls=%fused_computation.25 | convolution fusion | flops 5821816832 | bytes 19883264 | tf_op jit(solution)/shard_map/dot_general | solution.py:437
  247.6 3.1 convert_reduce_fusion
  252.4 2.9 convolution_convert_fusion.3
  255.3 28.4 %shard_map.425 = bf16[3,1232,768]{2,1,0:T(8,128)(2,1)S(1)} custom-call(bf16[1232,2304]{1,0:T(8,128)(2,1)S(1)} %bitcast.296, bf16[1232,2304]{1,0:T(8,128)(2,1)S(1)} %bitcast.296, bf16[1232,2304]{1,0:T(8,128)(2,1)S(1)} %bitcast.296, bf16[1232,768]{1,0:T(8,128)(2,1)S(1)} %copy-done.34, bf16[1232,768]{1,0:T(8,128)(2,1)S(1)} %convolution_convert_fusion.2.grad_ref, ...), custom_call_target="tpu_custom_call" | custom-call | flops 40000000000 | bytes 15138816 | tf_op jit(solution)/shard_map/pallas_call | solution.py:420
  293.7 3.6 fusion.18
  297.3 3.6 fusion.24
  301.0 5.5 %multiply_reduce_fusion.1 = (bf16[768]{0:T(1024)(128)(2,1)S(1)}, f32[1232]{0:T(1024)S(1)}, f32[1232]{0:T(1024)S(1)}, bf16[768]{0:T(1024)(128)(2,1)S(1)}, f32[1232,768]{1,0:T(8,128)S(1)}) fusion(f32[1232,768]{1,0:T(8,128)S(1)} %copy-done.39, f32[1232]{0:T(1024)S(1)} %copy-done.80, f32[1232]{0:T(1024)S(1)} %copy-done.78, f32[768]{0:T(1024)S(1)} %copy-done.82, ...), kind=kOutput, calls=%fused_computation.26 | convolution fusion | flops 1463730176 | bytes 18244224 | tf_op jit(solution)/shard_map/dot_general | solution.py:437
  317.0 13.8 %fusion.13 = bf16[1232,768]{1,0:T(8,128)(2,1)} fusion(f32[1232,768]{1,0:T(8,128)S(1)} %copy-done.43, bf16[3072,768]{1,0:T(8,128)(2,1)S(1)} %bitcast.286, f32[768]{0:T(1024)S(1)} %copy-done.87, f32[1232,3072]{1,0:T(8,128)} %fusion.82, f32[3072]{0:T(1024)S(1)} %add.266), kind=kOutput, calls=%fused_computation.41 | convolution fusion | flops 5853990912 | bytes 25549824 | tf_op jit(solution)/shard_map/dot_general | solution.py:433
  331.3 5.4 %pad_maximum_fusion = bf16[768,3072]{0,1:T(8,128)(2,1)} fusion(bf16[768,768]{0,1:T(8,128)(2,1)} %convolution_convert_fusion.3, bf16[768,768]{0,1:T(8,128)(2,1)} %fusion.29, bf16[768,768]{0,1:T(8,128)(2,1)} %fusion.25, bf16[768,768]{0,1:T(8,128)(2,1)} %fusion.26), kind=kLoop, calls=%fused_computation.14 | loop fusion | flops 18874368 | bytes 9437184 | tf_op jit(solution)/shard_map/concatenate | solution.py:549
  336.7 6.6 %copy.116 = bf16[768,3072]{1,0:T(8,128)(2,1)} copy(bf16[768,3072]{0,1:T(8,128)(2,1)} %pad_maximum_fusion) | data formatting | bytes 9437184 | tf_op jit(solution)/shard_map/concatenate | solution.py:549
  351.8 4.9 concatenate.134.whole
  356.7 4.8 shard_map.427
  362.0 10.7 %convolution_convert_fusion.1 = bf16[768,3072]{1,0:T(8,128)(2,1)S(1)} fusion(bf16[1232,3072]{1,0:T(8,128)(2,1)} %get-tuple-element.161, f32[1232,768]{1,0:T(8,128)} %copy-done.42, f32[768]{0:T(1024)S(1)} %copy-done.86, f32[768]{0:T(1024)S(1)} %get-tuple-element.126, f32[1232]{0:T(1024)S(1)} %add_rsqrt_fusion, f32[1232]{0:T(1024)S(1)} %broadcast_multiply_fusion.4), kind=kOutput, calls=%fused_computation.13 | convolution fusion | flops 5820395520 | bytes 16088704 | tf_op jit(solution)/shard_map/dot_general | solution.py:441
  376.0 5.6 %shard_map.426 = (bf16[1,3,160,160]{3,2,1,0:T(8,128)(2,1)}, bf16[1,3,240,240]{3,2,1,0:T(8,128)(2,1)}, bf16[1,3,384,384]{3,2,1,0:T(8,128)(2,1)}) custom-call(bf16[1232,768]{1,0:T(8,128)(2,1)S(1)} %copy-done.11, bf16[768,2048]{1,0:T(8,128)(2,1)S(1)} %bitcast.280), custom_call_target="tpu_custom_call" | custom-call | flops 5000000000 | bytes 10000000 | tf_op jit(solution)/shard_map/pallas_call | solution.py:273
  388.0 13.8 %collective-permute-done.29 = bf16[8,48,1024]{2,1,0:T(8,128)(2,1)S(1)} collective-permute-done((bf16[8,48,1024]{2,1,0:T(8,128)(2,1)S(1)}, bf16[8,48,1024]{2,1,0:T(8,128)(2,1)S(1)}, u32[]{:S(2)}, u32[]{:S(2)}) %collective-permute-start.29) | collective-permute-done | bytes 786464 | tf_op jit(solution)/shard_map/ppermute | solution.py:20
  407.8 6.1 %collective-permute-done.47 = bf16[4,192,768]{2,1,0:T(8,128)(2,1)S(1)} collective-permute-done((bf16[4,192,768]{2,1,0:T(8,128)(2,1)S(1)}, bf16[4,192,768]{2,1,0:T(8,128)(2,1)S(1)}, u32[]{:S(2)}, u32[]{:S(2)}) %collective-permute-start.47) | collective-permute-done | bytes 1179680 | tf_op jit(solution)/shard_map/ppermute | solution.py:20
  415.7 6.0 %collective-permute-done.30 = bf16[4,48,1024]{2,1,0:T(8,128)(2,1)S(1)} collective-permute-done((bf16[4,48,1024]{2,1,0:T(8,128)(2,1)S(1)}, bf16[4,48,1024]{2,1,0:T(8,128)(2,1)S(1)}, u32[]{:S(2)}, u32[]{:S(2)}) %collective-permute-start.30) | collective-permute-done | bytes 393248 | tf_op jit(solution)/shard_map/ppermute | solution.py:20
  424.0 5.7 %collective-permute-done.31 = bf16[2,48,1024]{2,1,0:T(8,128)(2,1)S(1)} collective-permute-done((bf16[2,48,1024]{2,1,0:T(8,128)(2,1)S(1)}, bf16[2,48,1024]{2,1,0:T(8,128)(2,1)S(1)}, u32[]{:S(2)}, u32[]{:S(2)}) %collective-permute-start.31) | collective-permute-done | bytes 196640 | tf_op jit(solution)/shard_map/ppermute | solution.py:20
  435.2 6.2 %collective-permute-done.32 = bf16[1,48,1024]{2,1,0:T(8,128)(2,1)S(1)} collective-permute-done((bf16[1,48,1024]{2,1,0:T(8,128)(2,1)S(1)}, bf16[1,48,1024]{2,1,0:T(8,128)(2,1)S(1)}, u32[]{:S(2)}, u32[]{:S(2)}) %collective-permute-start.32) | collective-permute-done | bytes 98336 | tf_op jit(solution)/shard_map/ppermute | solution.py:20
  444.2 3.4 collective-permute-start.49
  447.6 14.2 %collective-permute-done.33 = bf16[48,1024]{1,0:T(8,128)(2,1)S(1)} collective-permute-done((bf16[48,1024]{1,0:T(8,128)(2,1)S(1)}, bf16[48,1024]{1,0:T(8,128)(2,1)S(1)}, u32[]{:S(2)}, u32[]{:S(2)}) %collective-permute-start.33) | collective-permute-done | bytes 98336 | tf_op jit(solution)/shard_map/ppermute | solution.py:20
  476.4 3.0 convolution_add_fusion.5
  482.4 3.2 add_convert_fusion.4
  488.8 13.2 %collective-permute-done.36 = bf16[4,48,1536]{2,1,0:T(8,128)(2,1)S(1)} collective-permute-done((bf16[4,48,1536]{2,1,0:T(8,128)(2,1)S(1)}, bf16[4,48,1536]{2,1,0:T(8,128)(2,1)S(1)}, u32[]{:S(2)}, u32[]{:S(2)}) %collective-permute-start.36) | collective-permute-done | bytes 589856 | tf_op jit(solution)/shard_map/ppermute | solution.py:20
  503.7 7.0 %collective-permute-done.42 = bf16[4,48,1536]{2,1,0:T(8,128)(2,1)S(1)} collective-permute-done((bf16[4,48,1536]{2,1,0:T(8,128)(2,1)S(1)}, bf16[4,48,1536]{2,1,0:T(8,128)(2,1)S(1)}, u32[]{:S(2)}, u32[]{:S(2)}) %collective-permute-start.42) | collective-permute-done | bytes 589856 | tf_op jit(solution)/shard_map/ppermute | solution.py:20
  511.8 3.4 collective-permute-start.38
  515.3 4.1 collective-permute-done.43
  522.7 5.7 %collective-permute-done.44 = bf16[1,48,1536]{2,1,0:T(8,128)(2,1)S(1)} collective-permute-done((bf16[1,48,1536]{2,1,0:T(8,128)(2,1)S(1)}, bf16[1,48,1536]{2,1,0:T(8,128)(2,1)S(1)}, u32[]{:S(2)}, u32[]{:S(2)}) %collective-permute-start.44) | collective-permute-done | bytes 147488 | tf_op jit(solution)/shard_map/ppermute | solution.py:20
  530.6 3.1 collective-permute-done.45
  (444 shorter events, 174.9 us)
Async XLA Ops:
  1.5 20.3 %collective-permute-start.12 = (bf16[1,48,384]{2,1,0:T(8,128)(2,1)S(1)}, bf16[1,48,384]{2,1,0:T(8,128)(2,1)}, u32[]{:S(2)}, u32[]{:S(2)}) collective-permute-start(bf16[1,48,384]{2,1,0:T(8,128)(2,1)S(1)} %dynamic-slice_bitcast_fusion.3), channel_id=1, source_target_pairs={{0,8},{1,9},{2,10},{3,11},{4,12},{5,13},{6,14},{7,15},{8,0},{9,1},... | collective-permute-start | bytes 110600 | tf_op jit(solution)/shard_map/ppermute | solution.py:20
  6.4 36.6 %collective-permute-start.6 = (bf16[1,48,1152]{2,1,0:T(8,128)(2,1)S(1)}, bf16[1,48,1152]{2,1,0:T(8,128)(2,1)}, u32[]{:S(2)}, u32[]{:S(2)}) collective-permute-start(bf16[1,48,1152]{2,1,0:T(8,128)(2,1)S(1)} %dynamic-slice_bitcast_fusion.1), channel_id=1, source_target_pairs={{0,8},{1,9},{2,10},{3,11},{4,12},{5,13},{6,14},{7,15},{8,0},{9,1},... | collective-permute-start | bytes 331784 | tf_op jit(solution)/shard_map/ppermute | solution.py:20
  7.5 33.1 %collective-permute-start.18 = (bf16[1,48,1536]{2,1,0:T(8,128)(2,1)S(1)}, bf16[1,48,1536]{2,1,0:T(8,128)(2,1)}, u32[]{:S(2)}, u32[]{:S(2)}) collective-permute-start(bf16[1,48,1536]{2,1,0:T(8,128)(2,1)S(1)} %dynamic-slice_bitcast_fusion), channel_id=1, source_target_pairs={{0,8},{1,9},{2,10},{3,11},{4,12},{5,13},{6,14},{7,15},{8,0},{9,1},... | collective-permute-start | bytes 442376 | tf_op jit(solution)/shard_map/ppermute | solution.py:20
  10.4 34.8 %collective-permute-start.24 = (bf16[1,192,768]{2,1,0:T(8,128)(2,1)}, bf16[1,192,768]{2,1,0:T(8,128)(2,1)S(1)}, u32[]{:S(2)}, u32[]{:S(2)}) collective-permute-start(bf16[1,192,768]{2,1,0:T(8,128)(2,1)} %bitcast.314), channel_id=1, source_target_pairs={{0,8},{1,9},{2,10},{3,11},{4,12},{5,13},{6,14},{7,15},{8,0},{9,1},... | collective-permute-start | bytes 884744 | tf_op jit(solution)/shard_map/ppermute | solution.py:20
  18.9 18.7 %collective-permute-start = (bf16[1,48,1024]{2,1,0:T(8,128)(2,1)S(1)}, bf16[1,48,1024]{2,1,0:T(8,128)(2,1)S(1)}, u32[]{:S(2)}, u32[]{:S(2)}) collective-permute-start(bf16[1,48,1024]{2,1,0:T(8,128)(2,1)S(1)} %dynamic-slice_bitcast_fusion.2), channel_id=1, source_target_pairs={{0,8},{1,9},{2,10},{3,11},{4,12},{5,13},{6,14},{7,15},{8,0},{9,1},... | collective-permute-start | bytes 294920 | tf_op jit(solution)/shard_map/ppermute | solution.py:20
  22.6 15.6 %collective-permute-start.13 = (bf16[2,48,384]{2,1,0:T(8,128)(2,1)S(1)}, bf16[2,48,384]{2,1,0:T(8,128)(2,1)S(1)}, u32[]{:S(2)}, u32[]{:S(2)}) collective-permute-start(bf16[2,48,384]{2,1,0:T(8,128)(2,1)S(1)} %pad_maximum_fusion.18), channel_id=1, source_target_pairs={{0,4},{1,5},{2,6},{3,7},{4,0},{5,1},{6,2},{7,3},{8,12},{9,13},{10,... | collective-permute-start | bytes 221192 | tf_op jit(solution)/shard_map/ppermute | solution.py:20
  37.6 10.0 %collective-permute-start.1 = (bf16[2,48,1024]{2,1,0:T(8,128)(2,1)S(1)}, bf16[2,48,1024]{2,1,0:T(8,128)(2,1)S(1)}, u32[]{:S(2)}, u32[]{:S(2)}) collective-permute-start(bf16[2,48,1024]{2,1,0:T(8,128)(2,1)S(1)} %pad_maximum_fusion.16), channel_id=1, source_target_pairs={{0,4},{1,5},{2,6},{3,7},{4,0},{5,1},{6,2},{7,3},{8,12},{9,13},{10,... | collective-permute-start | bytes 589832 | tf_op jit(solution)/shard_map/ppermute | solution.py:20
  39.1 16.1 %collective-permute-start.14 = (bf16[4,48,384]{2,1,0:T(8,128)(2,1)S(1)}, bf16[4,48,384]{2,1,0:T(8,128)(2,1)S(1)}, u32[]{:S(2)}, u32[]{:S(2)}) collective-permute-start(bf16[4,48,384]{2,1,0:T(8,128)(2,1)S(1)} %pad_maximum_fusion.17), channel_id=1, source_target_pairs={{0,2},{1,3},{2,0},{3,1},{4,6},{5,7},{6,4},{7,5},{8,10},{9,11},{10,... | collective-permute-start | bytes 442376 | tf_op jit(solution)/shard_map/ppermute | solution.py:20
  41.6 10.0 %collective-permute-start.19 = (bf16[2,48,1536]{2,1,0:T(8,128)(2,1)S(1)}, bf16[2,48,1536]{2,1,0:T(8,128)(2,1)S(1)}, u32[]{:S(2)}, u32[]{:S(2)}) collective-permute-start(bf16[2,48,1536]{2,1,0:T(8,128)(2,1)S(1)} %pad_maximum_fusion.13), channel_id=1, source_target_pairs={{0,4},{1,5},{2,6},{3,7},{4,0},{5,1},{6,2},{7,3},{8,12},{9,13},{10,... | collective-permute-start | bytes 884744 | tf_op jit(solution)/shard_map/ppermute | solution.py:20
  44.7 13.3 %collective-permute-start.7 = (bf16[2,48,1152]{2,1,0:T(8,128)(2,1)}, bf16[2,48,1152]{2,1,0:T(8,128)(2,1)}, u32[]{:S(2)}, u32[]{:S(2)}) collective-permute-start(bf16[2,48,1152]{2,1,0:T(8,128)(2,1)} %pad_maximum_fusion.15), channel_id=1, source_target_pairs={{0,4},{1,5},{2,6},{3,7},{4,0},{5,1},{6,2},{7,3},{8,12},{9,13},{10,... | collective-permute-start | bytes 663560 | tf_op jit(solution)/shard_map/ppermute | solution.py:20
  46.2 21.0 %collective-permute-start.25 = (bf16[2,192,768]{2,1,0:T(8,128)(2,1)}, bf16[2,192,768]{2,1,0:T(8,128)(2,1)}, u32[]{:S(2)}, u32[]{:S(2)}) collective-permute-start(bf16[2,192,768]{2,1,0:T(8,128)(2,1)} %pad_maximum_fusion.9), channel_id=1, source_target_pairs={{0,4},{1,5},{2,6},{3,7},{4,0},{5,1},{6,2},{7,3},{8,12},{9,13},{10,... | collective-permute-start | bytes 1769480 | tf_op jit(solution)/shard_map/ppermute | solution.py:20
  48.4 14.7 %collective-permute-start.2 = (bf16[4,48,1024]{2,1,0:T(8,128)(2,1)}, bf16[4,48,1024]{2,1,0:T(8,128)(2,1)}, u32[]{:S(2)}, u32[]{:S(2)}) collective-permute-start(bf16[4,48,1024]{2,1,0:T(8,128)(2,1)} %pad_maximum_fusion.11), channel_id=1, source_target_pairs={{0,2},{1,3},{2,0},{3,1},{4,6},{5,7},{6,4},{7,5},{8,10},{9,11},{10,... | collective-permute-start | bytes 1179656 | tf_op jit(solution)/shard_map/ppermute | solution.py:20
  53.5 20.0 %collective-permute-start.20 = (bf16[4,48,1536]{2,1,0:T(8,128)(2,1)}, bf16[4,48,1536]{2,1,0:T(8,128)(2,1)}, u32[]{:S(2)}, u32[]{:S(2)}) collective-permute-start(bf16[4,48,1536]{2,1,0:T(8,128)(2,1)} %pad_maximum_fusion.8), channel_id=1, source_target_pairs={{0,2},{1,3},{2,0},{3,1},{4,6},{5,7},{6,4},{7,5},{8,10},{9,11},{10,... | collective-permute-start | bytes 1769480 | tf_op jit(solution)/shard_map/ppermute | solution.py:20
  58.0 28.4 %collective-permute-start.16 = (bf16[8,48,384]{2,1,0:T(8,128)(2,1)S(1)}, bf16[8,48,384]{2,1,0:T(8,128)(2,1)S(1)}, u32[]{:S(2)}, u32[]{:S(2)}) collective-permute-start(bf16[8,48,384]{2,1,0:T(8,128)(2,1)S(1)} %pad_maximum_fusion.12.refs_0_), channel_id=1, source_target_pairs={{0,1},{1,0},{2,3},{3,2},{4,5},{5,4},{6,7},{7,6},{8,9},{9,8},{10,11... | collective-permute-start | bytes 884744 | tf_op jit(solution)/shard_map/ppermute | solution.py:20
  62.8 20.1 %collective-permute-start.8 = (bf16[4,48,1152]{2,1,0:T(8,128)(2,1)S(1)}, bf16[4,48,1152]{2,1,0:T(8,128)(2,1)S(1)}, u32[]{:S(2)}, u32[]{:S(2)}) collective-permute-start(bf16[4,48,1152]{2,1,0:T(8,128)(2,1)S(1)} %pad_maximum_fusion.10), channel_id=1, source_target_pairs={{0,2},{1,3},{2,0},{3,1},{4,6},{5,7},{6,4},{7,5},{8,10},{9,11},{10,... | collective-permute-start | bytes 1327112 | tf_op jit(solution)/shard_map/ppermute | solution.py:20
  63.1 26.2 %collective-permute-start.17 = (bf16[8,48,384]{2,1,0:T(8,128)(2,1)S(1)}, bf16[8,48,384]{2,1,0:T(8,128)(2,1)S(1)}, u32[]{:S(2)}, u32[]{:S(2)}) collective-permute-start(bf16[8,48,384]{2,1,0:T(8,128)(2,1)S(1)} %collective-permute-done.15.refs_1_), channel_id=1, source_target_pairs={{0,1},{1,0},{2,3},{3,2},{4,5},{5,4},{6,7},{7,6},{8,9},{9,8},{10,11... | collective-permute-start | bytes 884744 | tf_op jit(solution)/shard_map/ppermute | solution.py:20
  67.2 22.1 %collective-permute-start.3 = (bf16[8,48,1024]{2,1,0:T(8,128)(2,1)S(1)}, bf16[8,48,1024]{2,1,0:T(8,128)(2,1)S(1)}, u32[]{:S(2)}, u32[]{:S(2)}) collective-permute-start(bf16[8,48,1024]{2,1,0:T(8,128)(2,1)S(1)} %pad_maximum_fusion.7.refs_0_), channel_id=1, source_target_pairs={{0,16},{16,0},{1,17},{17,1},{2,18},{18,2},{3,19},{19,3},{4,20},{20... | collective-permute-start | bytes 2359304 | tf_op jit(solution)/shard_map/ppermute | solution.py:20
  73.4 31.2 %collective-permute-start.26 = (bf16[4,192,768]{2,1,0:T(8,128)(2,1)}, bf16[4,192,768]{2,1,0:T(8,128)(2,1)}, u32[]{:S(2)}, u32[]{:S(2)}) collective-permute-start(bf16[4,192,768]{2,1,0:T(8,128)(2,1)} %pad_maximum_fusion.5), channel_id=1, source_target_pairs={{0,2},{1,3},{2,0},{3,1},{4,6},{5,7},{6,4},{7,5},{8,10},{9,11},{10,... | collective-permute-start | bytes 3538952 | tf_op jit(solution)/shard_map/ppermute | solution.py:20
  82.8 46.4 %collective-permute-start.21 = (bf16[8,48,1536]{2,1,0:T(8,128)(2,1)}, bf16[8,48,1536]{2,1,0:T(8,128)(2,1)}, u32[]{:S(2)}, u32[]{:S(2)}) collective-permute-start(bf16[8,48,1536]{2,1,0:T(8,128)(2,1)} %pad_maximum_fusion.4.refs_0_), channel_id=1, source_target_pairs={{0,16},{16,0},{1,17},{17,1},{2,18},{18,2},{3,19},{19,3},{4,20},{20... | collective-permute-start | bytes 3538952 | tf_op jit(solution)/shard_map/ppermute | solution.py:20
  86.4 42.8 %collective-permute-start.9 = (bf16[8,48,1152]{2,1,0:T(8,128)(2,1)}, bf16[8,48,1152]{2,1,0:T(8,128)(2,1)}, u32[]{:S(2)}, u32[]{:S(2)}) collective-permute-start(bf16[8,48,1152]{2,1,0:T(8,128)(2,1)} %pad_maximum_fusion.6.refs_0_), channel_id=1, source_target_pairs={{0,16},{16,0},{1,17},{17,1},{2,18},{18,2},{3,19},{19,3},{4,20},{20... | collective-permute-start | bytes 2654216 | tf_op jit(solution)/shard_map/ppermute | solution.py:20
  89.3 18.5 %collective-permute-start.4 = (bf16[8,48,1024]{2,1,0:T(8,128)(2,1)S(1)}, bf16[8,48,1024]{2,1,0:T(8,128)(2,1)S(1)}, u32[]{:S(2)}, u32[]{:S(2)}) collective-permute-start(bf16[8,48,1024]{2,1,0:T(8,128)(2,1)S(1)} %pad_maximum_fusion.7.refs_0_), channel_id=1, source_target_pairs={{0,1},{1,0},{2,3},{3,2},{4,5},{5,4},{6,7},{7,6},{8,9},{9,8},{10,11... | collective-permute-start | bytes 2359304 | tf_op jit(solution)/shard_map/ppermute | solution.py:20
  89.3 40.4 %collective-permute-start.5 = (bf16[8,48,1024]{2,1,0:T(8,128)(2,1)S(1)}, bf16[8,48,1024]{2,1,0:T(8,128)(2,1)S(1)}, u32[]{:S(2)}, u32[]{:S(2)}) collective-permute-start(bf16[8,48,1024]{2,1,0:T(8,128)(2,1)S(1)} %collective-permute-done.3.refs_1_), channel_id=1, source_target_pairs={{0,1},{1,0},{2,3},{3,2},{4,5},{5,4},{6,7},{7,6},{8,9},{9,8},{10,11... | collective-permute-start | bytes 2359304 | tf_op jit(solution)/shard_map/ppermute | solution.py:20
  104.6 46.9 %collective-permute-start.10 = (bf16[8,48,1152]{2,1,0:T(8,128)(2,1)}, bf16[8,48,1152]{2,1,0:T(8,128)(2,1)}, u32[]{:S(2)}, u32[]{:S(2)}) collective-permute-start(bf16[8,48,1152]{2,1,0:T(8,128)(2,1)} %pad_maximum_fusion.6.refs_0_), channel_id=1, source_target_pairs={{0,1},{1,0},{2,3},{3,2},{4,5},{5,4},{6,7},{7,6},{8,9},{9,8},{10,11... | collective-permute-start | bytes 2654216 | tf_op jit(solution)/shard_map/ppermute | solution.py:20
  107.7 74.6 %collective-permute-start.22 = (bf16[8,48,1536]{2,1,0:T(8,128)(2,1)}, bf16[8,48,1536]{2,1,0:T(8,128)(2,1)}, u32[]{:S(2)}, u32[]{:S(2)}) collective-permute-start(bf16[8,48,1536]{2,1,0:T(8,128)(2,1)} %pad_maximum_fusion.4.refs_0_), channel_id=1, source_target_pairs={{0,1},{1,0},{2,3},{3,2},{4,5},{5,4},{6,7},{7,6},{8,9},{9,8},{10,11... | collective-permute-start | bytes 3538952 | tf_op jit(solution)/shard_map/ppermute | solution.py:20
  129.2 22.4 %collective-permute-start.11 = (bf16[8,48,1152]{2,1,0:T(8,128)(2,1)}, bf16[8,48,1152]{2,1,0:T(8,128)(2,1)}, u32[]{:S(2)}, u32[]{:S(2)}) collective-permute-start(bf16[8,48,1152]{2,1,0:T(8,128)(2,1)} %collective-permute-done.9.refs_1_), channel_id=1, source_target_pairs={{0,1},{1,0},{2,3},{3,2},{4,5},{5,4},{6,7},{7,6},{8,9},{9,8},{10,11... | collective-permute-start | bytes 2654216 | tf_op jit(solution)/shard_map/ppermute | solution.py:20
  129.2 82.8 %collective-permute-start.27 = (bf16[8,192,768]{2,1,0:T(8,128)(2,1)}, bf16[8,192,768]{2,1,0:T(8,128)(2,1)}, u32[]{:S(2)}, u32[]{:S(2)}) collective-permute-start(bf16[8,192,768]{2,1,0:T(8,128)(2,1)} %pad_maximum_fusion.2.refs_0_), channel_id=1, source_target_pairs={{0,1},{1,0},{2,3},{3,2},{4,5},{5,4},{6,7},{7,6},{8,9},{9,8},{10,11... | collective-permute-start | bytes 7077896 | tf_op jit(solution)/shard_map/ppermute | solution.py:20
  129.7 52.7 %collective-permute-start.23 = (bf16[8,48,1536]{2,1,0:T(8,128)(2,1)}, bf16[8,48,1536]{2,1,0:T(8,128)(2,1)}, u32[]{:S(2)}, u32[]{:S(2)}) collective-permute-start(bf16[8,48,1536]{2,1,0:T(8,128)(2,1)} %collective-permute-done.21.refs_1_), channel_id=1, source_target_pairs={{0,1},{1,0},{2,3},{3,2},{4,5},{5,4},{6,7},{7,6},{8,9},{9,8},{10,11... | collective-permute-start | bytes 3538952 | tf_op jit(solution)/shard_map/ppermute | solution.py:20
  211.5 171.9 %collective-permute-start.46 = (bf16[8,192,768]{2,1,0:T(8,128)(2,1)}, bf16[8,192,768]{2,1,0:T(8,128)(2,1)}, u32[]{:S(2)}, u32[]{:S(2)}) collective-permute-start(bf16[8,192,768]{2,1,0:T(8,128)(2,1)} %get-tuple-element.52), channel_id=1, source_target_pairs={{0,1},{1,0},{2,3},{3,2},{4,5},{5,4},{6,7},{7,6},{8,9},{9,8},{10,11... | collective-permute-start | bytes 7077896 | tf_op jit(solution)/shard_map/ppermute | solution.py:20
  349.3 54.4 %collective-permute-start.34 = (bf16[8,48,3072]{2,1,0:T(8,128)(2,1)}, bf16[8,48,3072]{2,1,0:T(8,128)(2,1)}, u32[]{:S(2)}, u32[]{:S(2)}) collective-permute-start(bf16[8,48,3072]{2,1,0:T(8,128)(2,1)} %get-tuple-element.48), channel_id=1, source_target_pairs={{0,1},{1,0},{2,3},{3,2},{4,5},{5,4},{6,7},{7,6},{8,9},{9,8},{10,11... | collective-permute-start | bytes 7077896 | tf_op jit(solution)/shard_map/ppermute | solution.py:20
  361.5 20.0 %collective-permute-start.28 = (bf16[8,48,2048]{2,1,0:T(8,128)(2,1)S(1)}, bf16[8,48,2048]{2,1,0:T(8,128)(2,1)S(1)}, u32[]{:S(2)}, u32[]{:S(2)}) collective-permute-start(bf16[8,48,2048]{2,1,0:T(8,128)(2,1)S(1)} %get-tuple-element.46), channel_id=1, source_target_pairs={{0,1},{1,0},{2,3},{3,2},{4,5},{5,4},{6,7},{7,6},{8,9},{9,8},{10,11... | collective-permute-start | bytes 4718600 | tf_op jit(solution)/shard_map/ppermute | solution.py:20
  374.7 57.2 %collective-permute-start.40 = (bf16[8,48,3072]{2,1,0:T(8,128)(2,1)S(1)}, bf16[8,48,3072]{2,1,0:T(8,128)(2,1)S(1)}, u32[]{:S(2)}, u32[]{:S(2)}) collective-permute-start(bf16[8,48,3072]{2,1,0:T(8,128)(2,1)S(1)} %get-tuple-element.50), channel_id=1, source_target_pairs={{0,1},{1,0},{2,3},{3,2},{4,5},{5,4},{6,7},{7,6},{8,9},{9,8},{10,11... | collective-permute-start | bytes 7077896 | tf_op jit(solution)/shard_map/ppermute | solution.py:20
  381.8 20.0 %collective-permute-start.29 = (bf16[8,48,1024]{2,1,0:T(8,128)(2,1)S(1)}, bf16[8,48,1024]{2,1,0:T(8,128)(2,1)S(1)}, u32[]{:S(2)}, u32[]{:S(2)}) collective-permute-start(bf16[8,48,1024]{2,1,0:T(8,128)(2,1)S(1)} %add_convert_fusion.9), channel_id=1, source_target_pairs={{0,16},{16,0},{1,17},{17,1},{2,18},{18,2},{3,19},{19,3},{4,20},{20... | collective-permute-start | bytes 2359304 | tf_op jit(solution)/shard_map/ppermute | solution.py:20
  385.0 28.9 %collective-permute-start.47 = (bf16[4,192,768]{2,1,0:T(8,128)(2,1)S(1)}, bf16[4,192,768]{2,1,0:T(8,128)(2,1)S(1)}, u32[]{:S(2)}, u32[]{:S(2)}) collective-permute-start(bf16[4,192,768]{2,1,0:T(8,128)(2,1)S(1)} %fusion.37), channel_id=1, source_target_pairs={{0,2},{1,3},{2,0},{3,1},{4,6},{5,7},{6,4},{7,5},{8,10},{9,11},{10,... | collective-permute-start | bytes 3538952 | tf_op jit(solution)/shard_map/ppermute | solution.py:20
  402.3 19.4 %collective-permute-start.30 = (bf16[4,48,1024]{2,1,0:T(8,128)(2,1)S(1)}, bf16[4,48,1024]{2,1,0:T(8,128)(2,1)S(1)}, u32[]{:S(2)}, u32[]{:S(2)}) collective-permute-start(bf16[4,48,1024]{2,1,0:T(8,128)(2,1)S(1)} %slice_bitcast_fusion.17), channel_id=1, source_target_pairs={{0,2},{1,3},{2,0},{3,1},{4,6},{5,7},{6,4},{7,5},{8,10},{9,11},{10,... | collective-permute-start | bytes 1179656 | tf_op jit(solution)/shard_map/ppermute | solution.py:20
  406.3 76.1 %collective-permute-start.35 = (bf16[8,48,1536]{2,1,0:T(8,128)(2,1)}, bf16[8,48,1536]{2,1,0:T(8,128)(2,1)}, u32[]{:S(2)}, u32[]{:S(2)}) collective-permute-start(bf16[8,48,1536]{2,1,0:T(8,128)(2,1)} %add_convert_fusion.7), channel_id=1, source_target_pairs={{0,16},{16,0},{1,17},{17,1},{2,18},{18,2},{3,19},{19,3},{4,20},{20... | collective-permute-start | bytes 3538952 | tf_op jit(solution)/shard_map/ppermute | solution.py:20
  421.8 7.9 %collective-permute-start.31 = (bf16[2,48,1024]{2,1,0:T(8,128)(2,1)S(1)}, bf16[2,48,1024]{2,1,0:T(8,128)(2,1)S(1)}, u32[]{:S(2)}, u32[]{:S(2)}) collective-permute-start(bf16[2,48,1024]{2,1,0:T(8,128)(2,1)S(1)} %slice_bitcast_fusion.27), channel_id=1, source_target_pairs={{0,4},{1,5},{2,6},{3,7},{4,0},{5,1},{6,2},{7,3},{8,12},{9,13},{10,... | collective-permute-start | bytes 589832 | tf_op jit(solution)/shard_map/ppermute | solution.py:20
  422.8 20.5 %collective-permute-start.48 = (bf16[2,192,768]{2,1,0:T(8,128)(2,1)S(1)}, bf16[2,192,768]{2,1,0:T(8,128)(2,1)S(1)}, u32[]{:S(2)}, u32[]{:S(2)}) collective-permute-start(bf16[2,192,768]{2,1,0:T(8,128)(2,1)S(1)} %slice_bitcast_fusion.11), channel_id=1, source_target_pairs={{0,4},{1,5},{2,6},{3,7},{4,0},{5,1},{6,2},{7,3},{8,12},{9,13},{10,... | collective-permute-start | bytes 1769480 | tf_op jit(solution)/shard_map/ppermute | solution.py:20
  429.8 11.6 %collective-permute-start.32 = (bf16[1,48,1024]{2,1,0:T(8,128)(2,1)S(1)}, bf16[1,48,1024]{2,1,0:T(8,128)(2,1)S(1)}, u32[]{:S(2)}, u32[]{:S(2)}) collective-permute-start(bf16[1,48,1024]{2,1,0:T(8,128)(2,1)S(1)} %slice_bitcast_fusion.33), channel_id=1, source_target_pairs={{0,8},{1,9},{2,10},{3,11},{4,12},{5,13},{6,14},{7,15},{8,0},{9,1},... | collective-permute-start | bytes 294920 | tf_op jit(solution)/shard_map/ppermute | solution.py:20
  433.7 48.7 %collective-permute-start.41 = (bf16[8,48,1536]{2,1,0:T(8,128)(2,1)}, bf16[8,48,1536]{2,1,0:T(8,128)(2,1)}, u32[]{:S(2)}, u32[]{:S(2)}) collective-permute-start(bf16[8,48,1536]{2,1,0:T(8,128)(2,1)} %add_convert_fusion.5), channel_id=1, source_target_pairs={{0,16},{16,0},{1,17},{17,1},{2,18},{18,2},{3,19},{19,3},{4,20},{20... | collective-permute-start | bytes 3538952 | tf_op jit(solution)/shard_map/ppermute | solution.py:20
  441.4 20.4 %collective-permute-start.33 = (bf16[48,1024]{1,0:T(8,128)(2,1)S(1)}, bf16[48,1024]{1,0:T(8,128)(2,1)S(1)}, u32[]{:S(2)}, u32[]{:S(2)}) collective-permute-start(bf16[48,1024]{1,0:T(8,128)(2,1)S(1)} %fusion.78), channel_id=1, source_target_pairs={{0,16},{16,0},{1,17},{17,1},{2,18},{18,2},{3,19},{19,3},{4,20},{20... | collective-permute-start | bytes 294920 | tf_op jit(solution)/shard_map/ppermute | solution.py:20
  444.2 35.2 %collective-permute-start.49 = (bf16[1,192,768]{2,1,0:T(8,128)(2,1)}, bf16[1,192,768]{2,1,0:T(8,128)(2,1)}, u32[]{:S(2)}, u32[]{:S(2)}) collective-permute-start(bf16[1,192,768]{2,1,0:T(8,128)(2,1)} %slice_bitcast_fusion.21), channel_id=1, source_target_pairs={{0,8},{1,9},{2,10},{3,11},{4,12},{5,13},{6,14},{7,15},{8,0},{9,1},... | collective-permute-start | bytes 884744 | tf_op jit(solution)/shard_map/ppermute | solution.py:20
  480.6 7.3 %collective-permute-start.50 = (bf16[192,768]{1,0:T(8,128)(2,1)S(1)}, bf16[192,768]{1,0:T(8,128)(2,1)S(1)}, u32[]{:S(2)}, u32[]{:S(2)}) collective-permute-start(bf16[192,768]{1,0:T(8,128)(2,1)S(1)} %fusion.63), channel_id=1, source_target_pairs={{0,16},{16,0},{1,17},{17,1},{2,18},{18,2},{3,19},{19,3},{4,20},{20... | collective-permute-start | bytes 884744 | tf_op jit(solution)/shard_map/ppermute | solution.py:20
  485.7 16.3 %collective-permute-start.36 = (bf16[4,48,1536]{2,1,0:T(8,128)(2,1)S(1)}, bf16[4,48,1536]{2,1,0:T(8,128)(2,1)S(1)}, u32[]{:S(2)}, u32[]{:S(2)}) collective-permute-start(bf16[4,48,1536]{2,1,0:T(8,128)(2,1)S(1)} %slice_bitcast_fusion.15), channel_id=1, source_target_pairs={{0,2},{1,3},{2,0},{3,1},{4,6},{5,7},{6,4},{7,5},{8,10},{9,11},{10,... | collective-permute-start | bytes 1769480 | tf_op jit(solution)/shard_map/ppermute | solution.py:20
  486.7 24.0 %collective-permute-start.42 = (bf16[4,48,1536]{2,1,0:T(8,128)(2,1)S(1)}, bf16[4,48,1536]{2,1,0:T(8,128)(2,1)S(1)}, u32[]{:S(2)}, u32[]{:S(2)}) collective-permute-start(bf16[4,48,1536]{2,1,0:T(8,128)(2,1)S(1)} %slice_bitcast_fusion.13), channel_id=1, source_target_pairs={{0,2},{1,3},{2,0},{3,1},{4,6},{5,7},{6,4},{7,5},{8,10},{9,11},{10,... | collective-permute-start | bytes 1769480 | tf_op jit(solution)/shard_map/ppermute | solution.py:20
  502.2 9.6 %collective-permute-start.37 = (bf16[2,48,1536]{2,1,0:T(8,128)(2,1)S(1)}, bf16[2,48,1536]{2,1,0:T(8,128)(2,1)S(1)}, u32[]{:S(2)}, u32[]{:S(2)}) collective-permute-start(bf16[2,48,1536]{2,1,0:T(8,128)(2,1)S(1)} %slice_bitcast_fusion.25), channel_id=1, source_target_pairs={{0,4},{1,5},{2,6},{3,7},{4,0},{5,1},{6,2},{7,3},{8,12},{9,13},{10,... | collective-permute-start | bytes 884744 | tf_op jit(solution)/shard_map/ppermute | solution.py:20
  510.9 8.5 %collective-permute-start.43 = (bf16[2,48,1536]{2,1,0:T(8,128)(2,1)S(1)}, bf16[2,48,1536]{2,1,0:T(8,128)(2,1)S(1)}, u32[]{:S(2)}, u32[]{:S(2)}) collective-permute-start(bf16[2,48,1536]{2,1,0:T(8,128)(2,1)S(1)} %slice_bitcast_fusion.23), channel_id=1, source_target_pairs={{0,4},{1,5},{2,6},{3,7},{4,0},{5,1},{6,2},{7,3},{8,12},{9,13},{10,... | collective-permute-start | bytes 884744 | tf_op jit(solution)/shard_map/ppermute | solution.py:20
  511.8 10.2 %collective-permute-start.38 = (bf16[1,48,1536]{2,1,0:T(8,128)(2,1)S(1)}, bf16[1,48,1536]{2,1,0:T(8,128)(2,1)S(1)}, u32[]{:S(2)}, u32[]{:S(2)}) collective-permute-start(bf16[1,48,1536]{2,1,0:T(8,128)(2,1)S(1)} %slice_bitcast_fusion.31), channel_id=1, source_target_pairs={{0,8},{1,9},{2,10},{3,11},{4,12},{5,13},{6,14},{7,15},{8,0},{9,1},... | collective-permute-start | bytes 442376 | tf_op jit(solution)/shard_map/ppermute | solution.py:20
  519.5 8.9 %collective-permute-start.44 = (bf16[1,48,1536]{2,1,0:T(8,128)(2,1)S(1)}, bf16[1,48,1536]{2,1,0:T(8,128)(2,1)S(1)}, u32[]{:S(2)}, u32[]{:S(2)}) collective-permute-start(bf16[1,48,1536]{2,1,0:T(8,128)(2,1)S(1)} %slice_bitcast_fusion.29), channel_id=1, source_target_pairs={{0,8},{1,9},{2,10},{3,11},{4,12},{5,13},{6,14},{7,15},{8,0},{9,1},... | collective-permute-start | bytes 442376 | tf_op jit(solution)/shard_map/ppermute | solution.py:20
  (102 other events, 1048.7 us)
